TPU v7x, 512 devices: a whole 4x8x8 slice. The times are simulated.
512 devices in a mesh: stu: 32 (over y, z_lo, core), item: 16 (over z_hi, x).
Axes of the slice: x: 4, y: 8, z: 8 (z_hi: 4, z_lo: 2; z = z_hi * 2 + z_lo), core: 2. Of those that a mesh axis runs over, the one named last changes fastest.
Arguments:
- attempts: bfloat16 [65536, 12288], P('stu', 'item'), may hold values from -0.5 to 0.5
- item_factor: bfloat16 [12288, 64], P('item'), may hold values from -0.0546875 to 0.0546875
- core_factor: float32 [64, 64], replicated, may hold values from -1 to 1.5
- student_weights: float32 [128, 64], P('stu'), may hold values from 0.3 to 3
- blocks: int32 [32, 4], P('stu'), may hold values from 1 to 8, 16 in all within a row
Outputs:
- item_mttkrp: float32 [12288, 64], P('item')
- shared_mttkrp: float32 [64, 64], replicated
- student_mttkrp: float32 [128, 64], P('stu')
Inputs may be any that keep to these rules, and one draw needn't show every extreme that they name: Each row of blocks sums to 16, and some student of each row has exactly 8 blocks.
All inputs are finite; a program needn't handle non-finite values.
Results may differ from a plain program's by a relative error of at most 0.0003.
Values sent between devices are 32-bit elements; how exact they have to be, the bound alone decides.
No kernel may reach another device: no remote copies, remote signals or barrier semaphores. Data moves between devices by JAX's collectives and lax.ppermute only.
A program may use at most 64 MiB of HBM per device.

v0:
```python
import jax
import jax.numpy as jnp
from jax import lax
from jax.sharding import PartitionSpec as P

NS_STEPS = 6


HIGHEST = lax.Precision.HIGHEST


def owner_table(counts, row_total, group_rows):
    end_rows = jnp.cumsum(counts) * 128
    start_rows = end_rows - counts * 128
    places = jnp.arange(row_total // group_rows, dtype=jnp.int32) * group_rows
    inside = (places[:, None] >= start_rows[None, :]) & (places[:, None] < end_rows[None, :])
    return inside.astype(jnp.float32)


def polar_factor(target, owners, group_rows, combine):
    row_total, width = target.shape
    blocked = target.reshape(row_total // group_rows, group_rows, width)
    identity = jnp.eye(width, dtype=jnp.float32)

    def student_gram(blocked_now):
        grams = jnp.einsum("gla,glb->gab", blocked_now, blocked_now, precision=HIGHEST)
        return combine(jnp.einsum("gk,gab->kab", owners, grams, precision=HIGHEST))

    gram_now = student_gram(blocked)
    diagonal_sum = jnp.sum(gram_now * identity, axis=(1, 2))
    inverse_norm = 1.0 / jnp.sqrt(diagonal_sum + 1e-06)
    blocked = blocked * jnp.dot(owners, inverse_norm, precision=HIGHEST)[:, None, None]
    gram_now = gram_now * (inverse_norm * inverse_norm)[:, None, None]
    for iteration in range(NS_STEPS):
        if iteration > 0:
            gram_now = student_gram(blocked)
        factor = 1.5 * identity - 0.5 * gram_now
        spread = jnp.einsum("gk,kab->gab", owners, factor, precision=HIGHEST)
        blocked = jnp.einsum("gla,gab->glb", blocked, spread, precision=HIGHEST)
    return blocked.reshape(row_total, width)


def student_cross(orthogonal, raw_sums, owners, group_rows):
    row_total, width = raw_sums.shape
    left_side = orthogonal.reshape(row_total // group_rows, group_rows, width)
    right_side = raw_sums.reshape(row_total // group_rows, group_rows, width)
    grams = jnp.einsum("gla,glb->gab", left_side, right_side, precision=HIGHEST)
    return jnp.einsum("gk,gab->kab", owners, grams, precision=HIGHEST)


def scaled_target(raw_sums, owners, group_rows, weights_here, core_factor):
    row_total, width = raw_sums.shape
    row_scale = jnp.dot(owners, weights_here, precision=HIGHEST)
    scaled = raw_sums.reshape(row_total // group_rows, group_rows, width) * row_scale[:, None, :]
    return jnp.dot(scaled.reshape(row_total, width), core_factor.T, precision=HIGHEST)


def local(attempts, item_factor, core_factor, student_weights, blocks):
    row_total = attempts.shape[0]
    width = item_factor.shape[1]
    counts = blocks[0]
    full_owners = owner_table(counts, row_total, 128)
    local_sums = jnp.dot(attempts, item_factor, preferred_element_type=jnp.float32)
    raw_sums = lax.psum(local_sums, "item")
    target = scaled_target(raw_sums, full_owners, 128, student_weights, core_factor)
    orthogonal = polar_factor(target, full_owners, 128, lambda summand: summand)
    crossed = student_cross(orthogonal, raw_sums, full_owners, 128)
    row_scale = jnp.dot(full_owners, student_weights, precision=HIGHEST)
    lifted = jnp.dot(orthogonal, core_factor, precision=HIGHEST)
    lifted = lifted.reshape(row_total // 128, 128, width) * row_scale[:, None, :]
    weighted = lifted.reshape(row_total, width).astype(jnp.bfloat16)
    item_part = lax.dot_general(
        attempts, weighted, (((0,), (0,)), ((), ())), preferred_element_type=jnp.float32
    )
    shared_part = jnp.einsum("kab,kb->ab", crossed, student_weights, precision=HIGHEST)
    student_part = jnp.einsum("ab,kab->kb", core_factor, crossed, precision=HIGHEST)
    item_total, shared_total = lax.psum((item_part, shared_part), "stu")
    return (item_total, shared_total, student_part)


def solution(mesh):
    in_specs = (P("stu", "item"), P("item", None), P(), P("stu", None), P("stu", None))
    out_specs = (P("item", None), P(), P("stu", None))
    return jax.shard_map(local, mesh=mesh, in_specs=in_specs, out_specs=out_specs, check_vma=False)
```

profile of v0, /device:TPU:1, one launch (start us, length us, event | category | flops | bytes accessed | tf_op | source)
XLA Modules:
  0.0 437.6 jit_solution(16412960263734139279)
XLA Ops:
  7.3 1.8 copy-done
  9.1 2.8 fusion.73
  12.5 166.8 %all-reduce.3.cloned.1.call-done = f32[2048,64]{0,1:T(8,128)} async-done(((f32[2048,64]{0,1:T(8,128)}), f32[2048,64]{0,1:T(8,128)}) %all-reduce.3.cloned.1.call-update) | async-done | bytes 524304 | tf_op jit(solution)/shard_map/psum | solution.py:64
  179.5 1.8 fusion.11
  181.4 0.9 fusion.75
  182.3 0.8 multiply_reduce_fusion.2
  183.7 1.1 fusion.31
  184.8 0.9 fusion.76
  186.8 1.1 fusion.28
  187.9 0.9 fusion.77
  190.0 1.1 fusion.25
  191.0 0.9 fusion.78
  193.1 1.3 fusion.22
  194.3 0.9 fusion.79
  196.4 1.1 fusion.19
  197.5 0.9 fusion.80
  199.5 1.1 fusion.16
  200.6 0.8 copy-done.1
  202.0 1.3 convolution_bitcast_fusion
  203.4 2.1 fusion.8
  205.5 0.7 multiply_reduce_fusion.1
  206.2 111.2 %psum.23 = f32[64,64]{1,0:T(8,128)} all-reduce(f32[64,64]{1,0:T(8,128)S(1)} %bitcast.121), channel_id=1, replica_groups=mesh['stu'=32,'item'=16] {'stu'}, use_global_device_ids=true, to_apply=%region_4.5 | all-reduce | flops 4096 | bytes 32768 | tf_op jit(solution)/shard_map/psum | solution.py:77
  318.1 111.0 %all-reduce.5.cloned.1.call-done = f32[768,64]{0,1:T(8,128)} async-done(((f32[768,64]{0,1:T(8,128)}), f32[768,64]{0,1:T(8,128)}) %all-reduce.5.cloned.1.call-update) | async-done | bytes 196624 | tf_op jit(solution)/shard_map/psum | solution.py:77
  429.1 1.6 copy.97
  (37 shorter events, 8.1 us)
Async XLA Ops:
  7.2 1.9 copy-start
  7.2 4.7 %copy-start.4 = (s32[1,4]{1,0:T(1,128)S(1)}, s32[1,4]{1,0:T(1,128)}, u32[]{:S(2)}) copy-start(s32[1,4]{1,0:T(1,128)} %param.9) | copy-start | bytes 52
  7.2 5.0 %copy-start.3 = (f32[4,64]{1,0:T(4,128)S(1)}, f32[4,64]{1,0:T(4,128)}, u32[]{:S(2)}) copy-start(f32[4,64]{1,0:T(4,128)} %param.8) | copy-start | bytes 3076
  7.2 172.3 %copy-start.2 = (f32[64,64]{1,0:T(8,128)S(1)}, f32[64,64]{1,0:T(8,128)}, u32[]{:S(2)}) copy-start(f32[64,64]{1,0:T(8,128)} %param.7) | copy-start | bytes 49156
  7.2 172.1 %all-reduce.3.cloned.1.call-start = ((), (), s32[]{:S(2)}) async-start(), calls=%async_computation | async-start | bytes 1048576 | tf_op jit(solution)/shard_map/psum | solution.py:64
  11.8 417.3 %all-reduce.5.cloned.1.call-start = ((), (), s32[]{:S(2)}) async-start(), calls=%async_computation.1 | async-start | bytes 393216 | tf_op jit(solution)/shard_map/psum | solution.py:77
  200.6 0.8 copy-start.1
Sparse Core Ops, SparseCore 0:
  12.0 167.2 all-reduce.2
  203.5 225.5 all-reduce.4
where the time goes:
time: 438 us
  waiting for transfers between devices  278 us (63%)
  blocking collectives  111 us (25%)
  matrix products  28.7 us (7%)
  between operations  14.3 us (3%)
  local copies, waits for them, and re-layouts  4.52 us (1%)
    psum x1, waiting for transfers between devices, local(): raw_sums = lax.psum(local_sums, 'item')  167 us
    psum x1, blocking collectives, local(): item_total, shared_total = lax.psum((item_part, shared_part), 'stu')  111 us
    psum x1, waiting for transfers between devices, local(): item_total, shared_total = lax.psum((item_part, shared_part), 'stu')  111 us
  transfers between devices with their start and end apart: 2, of which 2 were waited for; matrix products, arithmetic and copies ran while one was open for 1% of the time, Pallas kernels for 0%

commit v1 on v0

v1 whole, which is shorter than its diff:
```python
import functools

import jax
import jax.numpy as jnp
from jax import lax
from jax.experimental import pallas as pl
from jax.experimental.pallas import tpu as pltpu
from jax.sharding import PartitionSpec as P

NS_STEPS = 6
BLOCK = 128
F32 = jnp.float32
BF16 = jnp.bfloat16
NN = (((1,), (0,)), ((), ()))
NT = (((1,), (1,)), ((), ()))
VMEM = pl.BlockSpec(memory_space=pltpu.VMEM)
SMEM = pl.BlockSpec(memory_space=pltpu.SMEM)


def project_kernel(factor_ref, rows_ref, out_ref):
    product = lax.dot_general(factor_ref[...], rows_ref[...], NT, preferred_element_type=F32)
    for piece in range(out_ref.shape[0]):
        out_ref[piece] = product[:, piece * BLOCK : (piece + 1) * BLOCK]


def project(attempts, factor_t, blocks_step):
    row_total, items = attempts.shape
    rank = factor_t.shape[0]
    count = row_total // BLOCK
    return pl.pallas_call(
        project_kernel,
        grid=(count // blocks_step,),
        in_specs=[
            pl.BlockSpec((rank, items), lambda i: (0, 0)),
            pl.BlockSpec((blocks_step * BLOCK, items), lambda i: (i, 0)),
        ],
        out_specs=pl.BlockSpec((blocks_step, rank, BLOCK), lambda i: (i, 0, 0)),
        out_shape=jax.ShapeDtypeStruct((count, rank, BLOCK), F32),
        name="project",
    )(factor_t, attempts)


def add_kernel(in_ref, out_ref):
    total = in_ref[0]
    for part in range(1, in_ref.shape[0]):
        total = total + in_ref[part]
    for part in range(out_ref.shape[0]):
        out_ref[part] = total


def add_and_copy(parts, name):
    return pl.pallas_call(
        add_kernel,
        in_specs=[VMEM],
        out_specs=VMEM,
        out_shape=jax.ShapeDtypeStruct(parts.shape, F32),
        name=name,
    )(parts)


def split(value):
    high = value.astype(BF16)
    return high, (value - high.astype(F32)).astype(BF16)


def dot3(left, right_parts, dims):
    rows = left.shape[0]
    high, low = split(left)
    right_high, right_low = right_parts
    both = lax.dot_general(
        jnp.concatenate([high, low], axis=0), right_high, dims, preferred_element_type=F32
    )
    cross = lax.dot_general(high, right_low, dims, preferred_element_type=F32)
    return both[:rows] + (both[rows:] + cross)


def solve_kernel(
    raw_ref, core_ref, weights_ref, counts_ref, attempts_ref,
    parts_ref, student_ref, spread_high, spread_low, held, arrived,
):
    count, rank, _ = raw_ref.shape
    students = weights_ref.shape[0]
    wide = students * rank
    load = pltpu.make_async_copy(attempts_ref, held, arrived)
    load.start()

    ends = [counts_ref[0, 0]]
    for student in range(1, students - 1):
        ends.append(ends[-1] + counts_ref[0, student])
    highs, lows = [], []
    for block in range(count):
        owner = sum((block >= end).astype(jnp.int32) for end in ends)
        value = raw_ref[block]
        high = value.astype(BF16).astype(F32)
        low = value - high
        highs.append(high.astype(BF16))
        lows.append(low.astype(BF16))
        for student in range(students):
            mine = (owner == student).astype(F32)
            place = (pl.ds(student * rank, rank), pl.ds(block * BLOCK, BLOCK))
            spread_high[place] = (high * mine).astype(BF16)
            spread_low[place] = (low * mine).astype(BF16)
    all_high = jnp.concatenate(highs, axis=1)
    all_low = jnp.concatenate(lows, axis=1)

    row_id = lax.broadcasted_iota(jnp.int32, (rank, wide), 0)
    col_id = lax.broadcasted_iota(jnp.int32, (rank, wide), 1)
    identity = (row_id == col_id % rank).astype(F32)
    student_id = col_id // rank
    on_diagonal = (
        lax.broadcasted_iota(jnp.int32, (wide, wide), 0) // rank
        == lax.broadcasted_iota(jnp.int32, (wide, wide), 1) // rank
    ).astype(F32)

    def diagonal(value):
        high = value.astype(BF16).astype(F32)
        low = value - high
        return tuple(
            (jnp.concatenate([half] * students, axis=0) * on_diagonal).astype(BF16)
            for half in (high, low)
        )

    both = lax.dot_general(
        jnp.concatenate([all_high, all_low], axis=0), spread_high[...], NT, preferred_element_type=F32
    )
    cross_term = lax.dot_general(all_high, spread_low[...], NT, preferred_element_type=F32)
    raw_gram = both[:rank] + (both[rank:] + cross_term)

    core = core_ref[...]
    scaled = [core * weights_ref[student : student + 1, :] for student in range(students)]
    lift = jnp.concatenate(scaled, axis=1)
    lift_t = jnp.concatenate([one.T for one in scaled], axis=1)
    lift_diagonal = diagonal(lift)

    half_way = dot3(lift, diagonal(raw_gram), NN)
    gram = dot3(half_way, lift_diagonal, NT)
    trace_row = jnp.sum(gram * identity, axis=0, keepdims=True)
    inverse = jnp.zeros((1, wide), F32)
    lane_student = student_id[:1]
    for student in range(students):
        here = lane_student == student
        trace = jnp.sum(jnp.where(here, trace_row, 0.0), axis=1, keepdims=True)
        inverse = jnp.where(here, 1.0 / jnp.sqrt(trace + 1e-06), inverse)
    gram = gram * (inverse * inverse)
    polynomial = None
    for iteration in range(NS_STEPS):
        factor = 1.5 * identity - 0.5 * gram
        factor_diagonal = diagonal(factor)
        last = iteration == NS_STEPS - 1
        if iteration == 0:
            moved = dot3(gram, factor_diagonal, NN)
            polynomial = factor
        elif last:
            polynomial = dot3(polynomial, factor_diagonal, NN)
        else:
            pair = dot3(jnp.concatenate([gram, polynomial], axis=0), factor_diagonal, NN)
            moved, polynomial = pair[:rank], pair[rank:]
        if not last:
            gram = dot3(moved, factor_diagonal, NN)
    polynomial = polynomial * inverse

    crossed = dot3(polynomial, diagonal(half_way), NN)
    lifted = dot3(polynomial, lift_diagonal, NN)
    apply = dot3(lift_t, diagonal(lifted), NN)

    shared = jnp.zeros((rank, rank), F32)
    for student in range(students):
        one = crossed[:, student * rank : (student + 1) * rank]
        shared = shared + one * weights_ref[student : student + 1, :]
        student_ref[student : student + 1, :] = jnp.sum(one * core, axis=0, keepdims=True)

    weighted = dot3(apply, (spread_high[...], spread_low[...]), NN).astype(BF16)
    load.wait()
    item_part = jnp.dot(weighted, held[...], preferred_element_type=F32)
    tiles = item_part.shape[1] // BLOCK
    for tile in range(tiles):
        parts_ref[tile * rank : (tile + 1) * rank, :] = item_part[:, tile * BLOCK : (tile + 1) * BLOCK]
    parts_ref[tiles * rank :, :] = jnp.zeros((parts_ref.shape[0] - tiles * rank, BLOCK), F32)
    parts_ref[tiles * rank : (tiles + 1) * rank, :rank] = shared


def solve(raw, core_factor, student_weights, blocks, attempts, part_rows):
    count, rank, _ = raw.shape
    students = student_weights.shape[0]
    wide = (students * rank, count * BLOCK)
    return pl.pallas_call(
        solve_kernel,
        in_specs=[VMEM, VMEM, VMEM, SMEM, pl.BlockSpec(memory_space=pl.ANY)],
        out_specs=[VMEM, VMEM],
        out_shape=[
            jax.ShapeDtypeStruct((part_rows, BLOCK), F32),
            jax.ShapeDtypeStruct((students, rank), F32),
        ],
        scratch_shapes=[
            pltpu.VMEM(wide, BF16),
            pltpu.VMEM(wide, BF16),
            pltpu.VMEM(attempts.shape, BF16),
            pltpu.SemaphoreType.DMA,
        ],
        compiler_params=pltpu.CompilerParams(vmem_limit_bytes=32 * 1024 * 1024),
        name="solve",
    )(raw, core_factor, student_weights, blocks, attempts)


def exchange(parts, axis):
    return lax.all_to_all(parts, axis, 0, 0, tiled=True)


def local(n_stu, attempts, item_factor, core_factor, student_weights, blocks):
    items, rank = item_factor.shape
    sums = project(attempts, item_factor.T, 4)
    sums = exchange(sums, "item")
    raw = exchange(add_and_copy(sums, "add_item"), "item")
    tiles = items // BLOCK
    step = 8 * n_stu
    part_rows = -(-(tiles + 1) * rank // step) * step
    parts, student_part = solve(raw, core_factor, student_weights, blocks, attempts, part_rows)
    parts = exchange(parts.reshape(n_stu, part_rows // n_stu, BLOCK), "stu")
    total = exchange(add_and_copy(parts, "add_stu"), "stu").reshape(part_rows, BLOCK)
    item_total = total[: tiles * rank].reshape(tiles, rank, BLOCK).transpose(1, 0, 2)
    shared_total = total[tiles * rank : (tiles + 1) * rank, :rank]
    return (item_total.reshape(rank, items).T, shared_total, student_part)


def solution(mesh):
    in_specs = (P("stu", "item"), P("item", None), P(), P("stu", None), P("stu", None))
    out_specs = (P("item", None), P(), P("stu", None))
    body = functools.partial(local, mesh.shape["stu"])
    return jax.shard_map(body, mesh=mesh, in_specs=in_specs, out_specs=out_specs, check_vma=False)
```

time: 438 us -> 106 us (0.24)
  waiting for transfers between devices: 278 us -> 0 us
  matrix products: 28.7 us -> 0 us
  blocking collectives: 111 us -> 89 us
  Pallas kernels: 0 us -> 14.4 us
  between operations: 14.3 us -> 0.7 us
    psum x2 -> x0, waiting for transfers between devices: 278 us -> none  [the longest x1 167 us: local(): raw_sums = lax.psum(local_sums, 'item')]
    psum x1 -> x0, blocking collectives: 111 us -> none  [local(): item_total, shared_total = lax.psum((item_part, shared_part), 'stu')]
    all_to_all x0 -> x4, blocking collectives: none -> 89 us  [exchange(): return lax.all_to_all(parts, axis, 0, 0, tiled=True)]
    dot_general x32 -> x0, matrix products: 28.7 us -> none  [the longest x6 6.68 us: polar_factor(): blocked = jnp.einsum('gla,gab->glb', blocked, spread, precision=HIGHEST)]
    pallas_call x0 -> x4, Pallas kernels: none -> 14.4 us  [the longest x1 6.27 us: solve(): pl.pallas_call(solve_kernel, in_specs=[VMEM, VMEM, VMEM, SMEM, pl.BlockSp...]
  transfers between devices with their start and end apart: 2 -> 0, of which waited for: 2 -> 0; matrix products, arithmetic and copies ran while one was open for 1% -> 0% of each run, Pallas kernels for 0% -> 0%
where the time goes in v1:
time: 106 us
  blocking collectives  89 us (84%)
  Pallas kernels  14.4 us (14%)
  local copies, waits for them, and re-layouts  1.48 us (1%)
    all_to_all x4, blocking collectives, exchange(): return lax.all_to_all(parts, axis, 0, 0, tiled=True)  89 us
    pallas_call x1, Pallas kernels, solve(): pl.pallas_call(solve_kernel, in_specs=[VMEM, VMEM, VMEM, SMEM, pl.BlockSp...  6.27 us
    pallas_call x1, Pallas kernels, project(): pl.pallas_call(project_kernel, grid=(count // blocks_step,), in_specs=[pl...  4.51 us
    pallas_call x2, Pallas kernels, add_and_copy(): pl.pallas_call(add_kernel, in_specs=[VMEM], out_specs=VMEM, out_shape=jax...  3.6 us

profile of v1, /device:TPU:1, one launch (start us, length us, event | category | flops | bytes accessed | tf_op | source)
XLA Modules:
  0.0 105.5 jit_solution(8378753168312683396)
XLA Ops:
  0.6 0.0 copy-start
  0.6 0.0 copy-start.1
  0.7 0.0 copy-start.2
  0.7 0.0 copy-start.3
  0.7 4.5 %project.1 = f32[16,64,128]{2,1,0:T(8,128)} custom-call(bf16[64,768]{1,0:T(8,128)(2,1)} %bitcast.17, bf16[2048,768]{1,0:T(8,128)(2,1)} %attempts_ref.1), custom_call_target="tpu_custom_call" | custom-call | tf_op jit(solution)/shard_map/project/pallas_call | solution.py:30
  5.2 26.4 %all_to_all.20.in_ref = f32[16,64,128]{2,1,0:T(8,128)} all-to-all(f32[16,64,128]{2,1,0:T(8,128)} %project.1), channel_id=1, replica_groups=mesh['stu'=32,'item'=16] {'item'}, dimensions={0} | all-to-all | bytes 1048576 | tf_op jit(solution)/shard_map/all_to_all | solution.py:206
  31.6 1.9 %add_item.1 = f32[16,64,128]{2,1,0:T(8,128)} custom-call(f32[16,64,128]{2,1,0:T(8,128)} %all_to_all.20.in_ref), custom_call_target="tpu_custom_call" | custom-call | tf_op jit(solution)/shard_map/add_item/pallas_call | solution.py:52
  33.5 19.3 %all_to_all.21.raw_ref = f32[16,64,128]{2,1,0:T(8,128)S(1)} all-to-all(f32[16,64,128]{2,1,0:T(8,128)} %add_item.1), channel_id=1, replica_groups=mesh['stu'=32,'item'=16] {'item'}, dimensions={0} | all-to-all | bytes 1048576 | tf_op jit(solution)/shard_map/all_to_all | solution.py:206
  52.8 0.0 copy-done
  52.8 0.0 copy-done.1
  52.8 0.0 copy-done.2
  52.8 0.0 copy-done.3
  52.8 6.3 %solve.1 = (f32[512,128]{1,0:T(8,128)S(1)}, f32[4,64]{1,0:T(4,128)}) custom-call(f32[16,64,128]{2,1,0:T(8,128)S(1)} %all_to_all.21.raw_ref, f32[64,64]{1,0:T(8,128)S(1)} %copy-done.1, f32[4,64]{1,0:T(4,128)S(1)} %copy-done.2, s32[1,4]{1,0:T(1,128)S(1)} %copy-done.3, bf16[2048,768]{1,0:T(8,128)(2,1)S(1)} %copy-done), custom_call_target="tpu_custom_call" | custom-call | tf_op jit(solution)/shard_map/solve/pallas_call | solution.py:186
  59.1 27.3 %all_to_all.22.in_ref = f32[32,16,128]{2,1,0:T(8,128)} all-to-all(f32[32,16,128]{2,1,0:T(8,128)S(1)} %bitcast.12), channel_id=1, replica_groups=mesh['stu'=32,'item'=16] {'stu'}, dimensions={0} | all-to-all | bytes 524288 | tf_op jit(solution)/shard_map/all_to_all | solution.py:206
  86.4 1.7 %add_stu.1 = f32[32,16,128]{2,1,0:T(8,128)} custom-call(f32[32,16,128]{2,1,0:T(8,128)} %all_to_all.22.in_ref), custom_call_target="tpu_custom_call" | custom-call | tf_op jit(solution)/shard_map/add_stu/pallas_call | solution.py:52
  88.1 16.0 %all_to_all.23 = f32[32,16,128]{2,1,0:T(8,128)S(1)} all-to-all(f32[32,16,128]{2,1,0:T(8,128)} %add_stu.1), channel_id=1, replica_groups=mesh['stu'=32,'item'=16] {'stu'}, dimensions={0} | all-to-all | bytes 524288 | tf_op jit(solution)/shard_map/all_to_all | solution.py:206
  104.1 0.6 slice.10
  104.7 0.1 copy.9
  104.8 0.7 copy.12
  (1 shorter events, 0.0 us)
Async XLA Ops:
  0.6 52.2 %copy-start = (bf16[2048,768]{1,0:T(8,128)(2,1)S(1)}, bf16[2048,768]{1,0:T(8,128)(2,1)}, u32[]{:S(2)}) copy-start(bf16[2048,768]{1,0:T(8,128)(2,1)} %attempts_ref.1) | copy-start | bytes 9437188
  0.6 52.2 %copy-start.1 = (f32[64,64]{1,0:T(8,128)S(1)}, f32[64,64]{1,0:T(8,128)}, u32[]{:S(2)}) copy-start(f32[64,64]{1,0:T(8,128)} %core_ref.1) | copy-start | bytes 49156
  0.7 52.2 %copy-start.2 = (f32[4,64]{1,0:T(4,128)S(1)}, f32[4,64]{1,0:T(4,128)}, u32[]{:S(2)}) copy-start(f32[4,64]{1,0:T(4,128)} %weights_ref.1) | copy-start | bytes 3076
  0.7 52.2 %copy-start.3 = (s32[1,4]{1,0:T(1,128)S(1)}, s32[1,4]{1,0:T(1,128)}, u32[]{:S(2)}) copy-start(s32[1,4]{1,0:T(1,128)} %counts_ref.1) | copy-start | bytes 52

commit v2 on v1

--- a/solution.py
+++ b/solution.py
@@ -9,6 +9,7 @@
 
 NS_STEPS = 6
 BLOCK = 128
+NEAR = 4
 F32 = jnp.float32
 BF16 = jnp.bfloat16
 NN = (((1,), (0,)), ((), ()))
@@ -17,27 +18,10 @@
 SMEM = pl.BlockSpec(memory_space=pltpu.SMEM)
 
 
-def project_kernel(factor_ref, rows_ref, out_ref):
-    product = lax.dot_general(factor_ref[...], rows_ref[...], NT, preferred_element_type=F32)
-    for piece in range(out_ref.shape[0]):
-        out_ref[piece] = product[:, piece * BLOCK : (piece + 1) * BLOCK]
-
-
-def project(attempts, factor_t, blocks_step):
+def project(attempts, factor_t):
     row_total, items = attempts.shape
-    rank = factor_t.shape[0]
-    count = row_total // BLOCK
-    return pl.pallas_call(
-        project_kernel,
-        grid=(count // blocks_step,),
-        in_specs=[
-            pl.BlockSpec((rank, items), lambda i: (0, 0)),
-            pl.BlockSpec((blocks_step * BLOCK, items), lambda i: (i, 0)),
-        ],
-        out_specs=pl.BlockSpec((blocks_step, rank, BLOCK), lambda i: (i, 0, 0)),
-        out_shape=jax.ShapeDtypeStruct((count, rank, BLOCK), F32),
-        name="project",
-    )(factor_t, attempts)
+    blocked = attempts.reshape(row_total // BLOCK, BLOCK, items)
+    return jnp.einsum("ri,bli->brl", factor_t, blocked, preferred_element_type=F32)
 
 
 def add_kernel(in_ref, out_ref):
@@ -48,12 +32,13 @@
         out_ref[part] = total
 
 
-def add_and_copy(parts, name):
+def add_and_copy(parts, copies, name):
     return pl.pallas_call(
         add_kernel,
         in_specs=[VMEM],
         out_specs=VMEM,
-        out_shape=jax.ShapeDtypeStruct(parts.shape, F32),
+        out_shape=jax.ShapeDtypeStruct((copies, *parts.shape[1:]), F32),
+        compiler_params=pltpu.CompilerParams(vmem_limit_bytes=2 * parts.size * 4 + 1024 * 1024),
         name=name,
     )(parts)
 
@@ -197,26 +182,34 @@
             pltpu.VMEM(attempts.shape, BF16),
             pltpu.SemaphoreType.DMA,
         ],
-        compiler_params=pltpu.CompilerParams(vmem_limit_bytes=32 * 1024 * 1024),
+        compiler_params=pltpu.CompilerParams(vmem_limit_bytes=16 * 1024 * 1024),
         name="solve",
     )(raw, core_factor, student_weights, blocks, attempts)
 
 
-def exchange(parts, axis):
-    return lax.all_to_all(parts, axis, 0, 0, tiled=True)
-
-
-def local(n_stu, attempts, item_factor, core_factor, student_weights, blocks):
+def exchange(parts, axis, groups=None):
+    return lax.all_to_all(parts, axis, 0, 0, tiled=True, axis_index_groups=groups)
+
+
+def sum_over_item(parts, n_item):
+    near = [[far * NEAR + i for i in range(NEAR)] for far in range(n_item // NEAR)]
+    distant = [[far * NEAR + i for far in range(n_item // NEAR)] for i in range(NEAR)]
+    shares = parts.reshape(NEAR, -1, BLOCK)
+    shares = exchange(shares, "item", near)
+    shares = exchange(add_and_copy(shares, n_item // NEAR, "add_near"), "item", distant)
+    shares = exchange(add_and_copy(shares, NEAR, "add_far"), "item", near)
+    return shares.reshape(parts.shape)
+
+
+def local(n_stu, n_item, attempts, item_factor, core_factor, student_weights, blocks):
     items, rank = item_factor.shape
-    sums = project(attempts, item_factor.T, 4)
-    sums = exchange(sums, "item")
-    raw = exchange(add_and_copy(sums, "add_item"), "item")
+    raw = sum_over_item(project(attempts, item_factor.T), n_item)
     tiles = items // BLOCK
     step = 8 * n_stu
     part_rows = -(-(tiles + 1) * rank // step) * step
     parts, student_part = solve(raw, core_factor, student_weights, blocks, attempts, part_rows)
     parts = exchange(parts.reshape(n_stu, part_rows // n_stu, BLOCK), "stu")
-    total = exchange(add_and_copy(parts, "add_stu"), "stu").reshape(part_rows, BLOCK)
+    total = exchange(add_and_copy(parts, n_stu, "add_stu"), "stu").reshape(part_rows, BLOCK)
     item_total = total[: tiles * rank].reshape(tiles, rank, BLOCK).transpose(1, 0, 2)
     shared_total = total[tiles * rank : (tiles + 1) * rank, :rank]
     return (item_total.reshape(rank, items).T, shared_total, student_part)
@@ -225,5 +218,5 @@
 def solution(mesh):
     in_specs = (P("stu", "item"), P("item", None), P(), P("stu", None), P("stu", None))
     out_specs = (P("item", None), P(), P("stu", None))
-    body = functools.partial(local, mesh.shape["stu"])
+    body = functools.partial(local, mesh.shape["stu"], mesh.shape["item"])
     return jax.shard_map(body, mesh=mesh, in_specs=in_specs, out_specs=out_specs, check_vma=False)

time: 106 us -> 99.4 us (0.938)
  Pallas kernels: 14.4 us -> 6.4 us
  matrix products: 0 us -> 2.95 us
  blocking collectives: 89 us -> 86.7 us
    pallas_call x1 -> x0, Pallas kernels: 4.51 us -> none  [project(): pl.pallas_call(project_kernel, grid=(count // blocks_step,), in_specs=[pl...]
    pallas_call x2 -> x3, Pallas kernels: 3.6 us -> 0.13 us  [add_and_copy(): pl.pallas_call(add_kernel, in_specs=[VMEM], out_specs=VMEM, out_shape=jax...]
    dot_general x0 -> x1, matrix products: none -> 2.95 us  [project(): jnp.einsum('ri,bli->brl', factor_t, blocked, preferred_element_type=F32)]
    all_to_all x4 -> x5, blocking collectives: 89 us -> 86.7 us  [exchange(): lax.all_to_all(parts, axis, 0, 0, tiled=True, axis_index_groups=groups)]
where the time goes in v2:
time: 99.4 us; the launch traced here: 99.1 us
  blocking collectives  86.7 us (87%)
  Pallas kernels  6.4 us (6%)
  matrix products  2.95 us (3%)
  local copies, waits for them, and re-layouts  2.38 us (2%)
    all_to_all x5, blocking collectives, exchange(): lax.all_to_all(parts, axis, 0, 0, tiled=True, axis_index_groups=groups)  86.7 us
    pallas_call x1, Pallas kernels, solve(): pl.pallas_call(solve_kernel, in_specs=[VMEM, VMEM, VMEM, SMEM, pl.BlockSp...  6.27 us
    dot_general x1, matrix products, project(): jnp.einsum('ri,bli->brl', factor_t, blocked, preferred_element_type=F32)  2.95 us

profile of v2, /device:TPU:1, one launch (start us, length us, event | category | flops | bytes accessed | tf_op | source)
XLA Modules:
  0.0 99.1 jit_solution(15905176889396023778)
XLA Ops:
  0.6 0.0 copy-start
  0.6 0.9 copy-done
  1.5 2.9 %fusion = f32[16,128,64]{1,2,0:T(8,128)S(1)} fusion(bf16[16,128,768]{2,1,0:T(8,128)(2,1)} %bitcast.20, bf16[768,64]{0,1:T(8,128)(2,1)S(1)} %copy-done), kind=kOutput, calls=%fused_computation.1 | convolution fusion | flops 201326592 | bytes 3768320 | tf_op jit(solution)/shard_map/ri,bli->brl/dot_general | solution.py:24
  4.5 0.0 copy-start.1
  4.5 0.0 copy-start.2
  4.5 0.0 copy-start.3
  4.5 0.0 copy-start.4
  4.5 11.8 %all_to_all.25.in_ref = f32[4,256,128]{2,1,0:T(8,128)S(1)} all-to-all(f32[4,256,128]{2,1,0:T(8,128)S(1)} %bitcast.23), channel_id=1, replica_groups={{0,1,2,3},{4,5,6,7},{8,9,10,11},{12,13,14,15},{16,17,18,19},{20,21,22,2..., dimensions={0} | all-to-all | bytes 1048576 | tf_op jit(solution)/shard_map/all_to_all | solution.py:191
  16.4 23.2 %all_to_all.26.in_ref = f32[4,256,128]{2,1,0:T(8,128)S(1)} all-to-all(f32[4,256,128]{2,1,0:T(8,128)S(1)} %add_near.1), channel_id=1, replica_groups={{0,4,8,12},{1,5,9,13},{2,6,10,14},{3,7,11,15},{16,20,24,28},{17,21,25,2..., dimensions={0} | all-to-all | bytes 1048576 | tf_op jit(solution)/shard_map/all_to_all | solution.py:191
  39.7 9.3 %all_to_all.27 = f32[4,256,128]{2,1,0:T(8,128)S(1)} all-to-all(f32[4,256,128]{2,1,0:T(8,128)S(1)} %add_far.1), channel_id=1, replica_groups={{0,1,2,3},{4,5,6,7},{8,9,10,11},{12,13,14,15},{16,17,18,19},{20,21,22,2..., dimensions={0} | all-to-all | bytes 1048576 | tf_op jit(solution)/shard_map/all_to_all | solution.py:191
  49.0 0.0 copy-done.1
  49.0 0.0 copy-done.2
  49.0 0.0 copy-done.3
  49.0 0.0 copy-done.4
  49.0 6.3 %solve.1 = (f32[512,128]{1,0:T(8,128)S(1)}, f32[4,64]{1,0:T(4,128)}) custom-call(f32[16,64,128]{2,1,0:T(8,128)S(1)} %bitcast.21, f32[64,64]{1,0:T(8,128)S(1)} %copy-done.2, f32[4,64]{1,0:T(4,128)S(1)} %copy-done.3, s32[1,4]{1,0:T(1,128)S(1)} %copy-done.4, bf16[2048,768]{1,0:T(8,128)(2,1)S(1)} %copy-done.1), custom_call_target="tpu_custom_call" | custom-call | tf_op jit(solution)/shard_map/solve/pallas_call | solution.py:171
  55.3 26.9 %all_to_all.28.in_ref = f32[32,16,128]{2,1,0:T(8,128)S(1)} all-to-all(f32[32,16,128]{2,1,0:T(8,128)S(1)} %bitcast.22), channel_id=1, replica_groups=mesh['stu'=32,'item'=16] {'stu'}, dimensions={0} | all-to-all | bytes 524288 | tf_op jit(solution)/shard_map/all_to_all | solution.py:191
  82.2 0.1 add_stu.1
  82.2 15.4 %all_to_all.29 = f32[32,16,128]{2,1,0:T(8,128)S(1)} all-to-all(f32[32,16,128]{2,1,0:T(8,128)S(1)} %add_stu.1), channel_id=1, replica_groups=mesh['stu'=32,'item'=16] {'stu'}, dimensions={0} | all-to-all | bytes 524288 | tf_op jit(solution)/shard_map/all_to_all | solution.py:191
  97.6 0.6 slice.10
  98.3 0.1 copy.9
  98.4 0.7 copy.12
  (3 shorter events, 0.1 us)
Async XLA Ops:
  0.6 0.9 copy-start
  4.5 44.5 %copy-start.1 = (bf16[2048,768]{1,0:T(8,128)(2,1)S(1)}, bf16[2048,768]{1,0:T(8,128)(2,1)}, u32[]{:S(2)}) copy-start(bf16[2048,768]{1,0:T(8,128)(2,1)} %attempts_ref.1) | copy-start | bytes 9437188
  4.5 44.5 %copy-start.2 = (f32[64,64]{1,0:T(8,128)S(1)}, f32[64,64]{1,0:T(8,128)}, u32[]{:S(2)}) copy-start(f32[64,64]{1,0:T(8,128)} %core_ref.1) | copy-start | bytes 49156
  4.5 44.5 %copy-start.3 = (f32[4,64]{1,0:T(4,128)S(1)}, f32[4,64]{1,0:T(4,128)}, u32[]{:S(2)}) copy-start(f32[4,64]{1,0:T(4,128)} %weights_ref.1) | copy-start | bytes 3076
  4.5 44.5 %copy-start.4 = (s32[1,4]{1,0:T(1,128)S(1)}, s32[1,4]{1,0:T(1,128)}, u32[]{:S(2)}) copy-start(s32[1,4]{1,0:T(1,128)} %counts_ref.1) | copy-start | bytes 52

commit v3 on v2

v3 whole, which is shorter than its diff:
```python
import functools

import jax
import jax.numpy as jnp
from jax import lax
from jax.experimental import pallas as pl
from jax.experimental.pallas import tpu as pltpu
from jax.sharding import PartitionSpec as P

NS_STEPS = 6
PROJECT_VMEM = 56 * 1024 * 1024
BLOCK = 128
NEAR = 4
F32 = jnp.float32
BF16 = jnp.bfloat16
NN = (((1,), (0,)), ((), ()))
NT = (((1,), (1,)), ((), ()))
VMEM = pl.BlockSpec(memory_space=pltpu.VMEM)
SMEM = pl.BlockSpec(memory_space=pltpu.SMEM)


def project_kernel(factor_ref, rows_ref, out_ref, factor, held, arrived, factor_arrived):
    chunks = arrived.shape[0]
    rows = held.shape[0] // chunks
    factor_load = pltpu.make_async_copy(factor_ref, factor, factor_arrived)
    factor_load.start()
    loads = []
    for chunk in range(chunks):
        place = pl.ds(chunk * rows, rows)
        loads.append(pltpu.make_async_copy(rows_ref.at[place], held.at[place], arrived.at[chunk]))
        loads[-1].start()
    factor_load.wait()
    pieces = rows // BLOCK
    for chunk in range(chunks):
        loads[chunk].wait()
        here = held[chunk * rows : (chunk + 1) * rows, :]
        product = lax.dot_general(factor[...], here, NT, preferred_element_type=F32)
        for piece in range(pieces):
            out_ref[chunk * pieces + piece] = product[:, piece * BLOCK : (piece + 1) * BLOCK]


def project(attempts, factor_t, chunks):
    row_total, items = attempts.shape
    rank = factor_t.shape[0]
    return pl.pallas_call(
        project_kernel,
        in_specs=[pl.BlockSpec(memory_space=pl.ANY)] * 2,
        out_specs=VMEM,
        out_shape=pltpu.VMEM((row_total // BLOCK, rank, BLOCK), F32),
        scratch_shapes=[
            pltpu.VMEM(factor_t.shape, BF16),
            pltpu.VMEM(attempts.shape, BF16),
            pltpu.SemaphoreType.DMA((chunks,)),
            pltpu.SemaphoreType.DMA,
        ],
        compiler_params=pltpu.CompilerParams(vmem_limit_bytes=PROJECT_VMEM),
        name="project",
    )(factor_t, attempts)


def add_kernel(in_ref, out_ref):
    total = in_ref[0]
    for part in range(1, in_ref.shape[0]):
        total = total + in_ref[part]
    for part in range(out_ref.shape[0]):
        out_ref[part] = total


def add_and_copy(parts, copies, name):
    return pl.pallas_call(
        add_kernel,
        in_specs=[VMEM],
        out_specs=VMEM,
        out_shape=jax.ShapeDtypeStruct((copies, *parts.shape[1:]), F32),
        compiler_params=pltpu.CompilerParams(vmem_limit_bytes=2 * parts.size * 4 + 1024 * 1024),
        name=name,
    )(parts)


def split(value):
    high = value.astype(BF16)
    return high, (value - high.astype(F32)).astype(BF16)


def dot3(left, right_parts, dims):
    rows = left.shape[0]
    high, low = split(left)
    right_high, right_low = right_parts
    both = lax.dot_general(
        jnp.concatenate([high, low], axis=0), right_high, dims, preferred_element_type=F32
    )
    cross = lax.dot_general(high, right_low, dims, preferred_element_type=F32)
    return both[:rows] + (both[rows:] + cross)


def solve_kernel(
    raw_ref, core_ref, weights_ref, counts_ref, attempts_ref,
    parts_ref, student_ref, halves, grams, lifts,
):
    count, rank, _ = raw_ref.shape
    students = weights_ref.shape[0]
    wide = students * rank

    ends = [counts_ref[0, 0]]
    for student in range(1, students - 1):
        ends.append(ends[-1] + counts_ref[0, student])
    owners = [sum((block >= end).astype(jnp.int32) for end in ends) for block in range(count)]
    grams[...] = jnp.zeros(grams.shape, F32)
    for block in range(count):
        both = jnp.concatenate(split(raw_ref[block]), axis=0)
        halves[block] = both
        grams[owners[block]] += lax.dot_general(both, both, NT, preferred_element_type=F32)

    row_id = lax.broadcasted_iota(jnp.int32, (rank, wide), 0)
    col_id = lax.broadcasted_iota(jnp.int32, (rank, wide), 1)
    identity = (row_id == col_id % rank).astype(F32)
    student_id = col_id // rank
    on_diagonal = (
        lax.broadcasted_iota(jnp.int32, (wide, wide), 0) // rank
        == lax.broadcasted_iota(jnp.int32, (wide, wide), 1) // rank
    ).astype(F32)

    def diagonal(value):
        high = value.astype(BF16).astype(F32)
        low = value - high
        return tuple(
            (jnp.concatenate([half] * students, axis=0) * on_diagonal).astype(BF16)
            for half in (high, low)
        )

    def beside(parts):
        return jnp.concatenate(parts, axis=1)

    core = core_ref[...]
    scaled = [core * weights_ref[student : student + 1, :] for student in range(students)]
    lift_t = beside([one.T for one in scaled])
    lift_diagonal = diagonal(beside(scaled))

    raw_grams = []
    for student in range(students):
        terms = grams[student]
        rows = terms[:rank] + terms[rank:]
        raw_grams.append(rows[:, :rank] + rows[:, rank:])
    raw_diagonal = diagonal(beside(raw_grams))
    gram = dot3(dot3(beside(scaled), raw_diagonal, NN), lift_diagonal, NT)
    trace_row = jnp.sum(gram * identity, axis=0, keepdims=True)
    inverse = jnp.zeros((1, wide), F32)
    lane_student = student_id[:1]
    for student in range(students):
        here = lane_student == student
        trace = jnp.sum(jnp.where(here, trace_row, 0.0), axis=1, keepdims=True)
        inverse = jnp.where(here, 1.0 / jnp.sqrt(trace + 1e-06), inverse)
    gram = gram * (inverse * inverse)
    polynomial = lift_t * inverse
    for iteration in range(NS_STEPS):
        factor_diagonal = diagonal(1.5 * identity - 0.5 * gram)
        if iteration == NS_STEPS - 1:
            polynomial = dot3(polynomial, factor_diagonal, NN)
        else:
            pair = dot3(jnp.concatenate([gram, polynomial], axis=0), factor_diagonal, NN)
            polynomial = pair[rank:]
            gram = dot3(pair[:rank], factor_diagonal, NN)

    apply = dot3(polynomial, lift_diagonal, NN)
    for student in range(students):
        high, low = split(apply[:, student * rank : (student + 1) * rank])
        lifts[student] = jnp.concatenate([beside([high, high]), beside([low, low])], axis=0)
    weighted = []
    for block in range(count):
        terms = jnp.dot(lifts[owners[block]], halves[block], preferred_element_type=F32)
        weighted.append((terms[:rank] + terms[rank:]).astype(BF16))
    item_part = jnp.dot(beside(weighted), attempts_ref[...], preferred_element_type=F32)

    turned = beside([polynomial[:, k * rank : (k + 1) * rank].T for k in range(students)])
    crossed = dot3(turned, raw_diagonal, NN)
    shared = jnp.zeros((rank, rank), F32)
    for student in range(students):
        one = crossed[:, student * rank : (student + 1) * rank]
        shared = shared + one * weights_ref[student : student + 1, :]
        student_ref[student : student + 1, :] = jnp.sum(one * core, axis=0, keepdims=True)

    tiles = item_part.shape[1] // BLOCK
    for tile in range(tiles):
        parts_ref[tile * rank : (tile + 1) * rank, :] = item_part[:, tile * BLOCK : (tile + 1) * BLOCK]
    parts_ref[tiles * rank :, :] = jnp.zeros((parts_ref.shape[0] - tiles * rank, BLOCK), F32)
    parts_ref[tiles * rank : (tiles + 1) * rank, :rank] = shared


def solve(raw, core_factor, student_weights, blocks, attempts, part_rows):
    count, rank, _ = raw.shape
    students = student_weights.shape[0]
    return pl.pallas_call(
        solve_kernel,
        in_specs=[VMEM, VMEM, VMEM, SMEM, VMEM],
        out_specs=[VMEM, VMEM],
        out_shape=[
            jax.ShapeDtypeStruct((part_rows, BLOCK), F32),
            jax.ShapeDtypeStruct((students, rank), F32),
        ],
        scratch_shapes=[
            pltpu.VMEM((count, 2 * rank, BLOCK), BF16),
            pltpu.VMEM((students, 2 * rank, 2 * rank), F32),
            pltpu.VMEM((students, 2 * rank, 2 * rank), BF16),
        ],
        compiler_params=pltpu.CompilerParams(vmem_limit_bytes=16 * 1024 * 1024),
        name="solve",
    )(raw, core_factor, student_weights, blocks, attempts)


def finish_kernel(total_ref, item_ref, shared_ref):
    rank, items = item_ref.shape
    for tile in range(items // BLOCK):
        item_ref[:, tile * BLOCK : (tile + 1) * BLOCK] = total_ref[tile * rank : (tile + 1) * rank, :]
    last = items // BLOCK * rank
    shared_ref[...] = total_ref[last : last + rank, :rank]


def finish(total, rank, items):
    return pl.pallas_call(
        finish_kernel,
        in_specs=[VMEM],
        out_specs=[VMEM, VMEM],
        out_shape=[
            jax.ShapeDtypeStruct((rank, items), F32),
            jax.ShapeDtypeStruct((rank, rank), F32),
        ],
        compiler_params=pltpu.CompilerParams(vmem_limit_bytes=2 * 1024 * 1024),
        name="finish",
    )(total)


def exchange(parts, axis, groups=None):
    return lax.all_to_all(parts, axis, 0, 0, tiled=True, axis_index_groups=groups)


def sum_over_item(parts, n_item):
    near = [[far * NEAR + i for i in range(NEAR)] for far in range(n_item // NEAR)]
    distant = [[far * NEAR + i for far in range(n_item // NEAR)] for i in range(NEAR)]
    shares = parts.reshape(NEAR, -1, BLOCK)
    shares = exchange(shares, "item", near)
    shares = exchange(add_and_copy(shares, n_item // NEAR, "add_near"), "item", distant)
    shares = exchange(add_and_copy(shares, NEAR, "add_far"), "item", near)
    return shares.reshape(parts.shape)


def local(n_stu, n_item, attempts, item_factor, core_factor, student_weights, blocks):
    items, rank = item_factor.shape
    raw = sum_over_item(project(attempts, item_factor.T, 2), n_item)
    tiles = items // BLOCK
    step = 8 * n_stu
    part_rows = -(-(tiles + 1) * rank // step) * step
    parts, student_part = solve(raw, core_factor, student_weights, blocks, attempts, part_rows)
    parts = exchange(parts.reshape(n_stu, part_rows // n_stu, BLOCK), "stu")
    total = exchange(add_and_copy(parts, n_stu, "add_stu"), "stu").reshape(part_rows, BLOCK)
    item_total, shared_total = finish(total, rank, items)
    return (item_total.T, shared_total, student_part)


def solution(mesh):
    in_specs = (P("stu", "item"), P("item", None), P(), P("stu", None), P("stu", None))
    out_specs = (P("item", None), P(), P("stu", None))
    body = functools.partial(local, mesh.shape["stu"], mesh.shape["item"])
    return jax.shard_map(body, mesh=mesh, in_specs=in_specs, out_specs=out_specs, check_vma=False)
```

time: 99.4 us -> 96.7 us (0.973)
  matrix products: 2.95 us -> 0 us
  Pallas kernels: 6.4 us -> 9.06 us
  local copies, waits for them, and re-layouts: 2.38 us -> 0.03 us
    dot_general x1 -> x0, matrix products: 2.95 us -> none  [project(): jnp.einsum('ri,bli->brl', factor_t, blocked, preferred_element_type=F32)]
    pallas_call x1 -> x3, Pallas kernels: 6.27 us -> 8.93 us  [the longest x1 5.6 us: solve(): pl.pallas_call(solve_kernel, in_specs=[VMEM, VMEM, VMEM, SMEM, VMEM], out...]
    unnamed x11 -> x8, local copies, waits for them, and re-layouts: 1.63 us -> 0.03 us
where the time goes in v3:
time: 96.7 us; the launch traced here: 96.4 us
  blocking collectives  86.6 us (90%)
  Pallas kernels  9.06 us (9%)
    all_to_all x5, blocking collectives, exchange(): lax.all_to_all(parts, axis, 0, 0, tiled=True, axis_index_groups=groups)  86.6 us
    pallas_call x1, Pallas kernels, solve(): pl.pallas_call(solve_kernel, in_specs=[VMEM, VMEM, VMEM, SMEM, VMEM], out...  5.6 us
    pallas_call x1, Pallas kernels, project(): pl.pallas_call(project_kernel, in_specs=[pl.BlockSpec(memory_space=pl.ANY...  2.63 us

profile of v3, /device:TPU:1, one launch (start us, length us, event | category | flops | bytes accessed | tf_op | source)
XLA Modules:
  0.0 96.4 jit_solution(17203390366703058233)
XLA Ops:
  0.6 2.6 %project.1 = f32[16,64,128]{2,1,0:T(8,128)S(1)} custom-call(bf16[64,768]{1,0:T(8,128)(2,1)} %bitcast.10, bf16[2048,768]{1,0:T(8,128)(2,1)} %attempts_ref.1), custom_call_target="tpu_custom_call" | custom-call | tf_op jit(solution)/shard_map/project/pallas_call | solution.py:45
  3.3 0.0 copy-start
  3.3 0.0 copy-start.1
  3.3 0.0 copy-start.2
  3.3 0.0 copy-start.3
  3.3 11.8 %all_to_all.25.in_ref = f32[4,256,128]{2,1,0:T(8,128)S(1)} all-to-all(f32[4,256,128]{2,1,0:T(8,128)S(1)} %bitcast.7), channel_id=1, replica_groups={{0,1,2,3},{4,5,6,7},{8,9,10,11},{12,13,14,15},{16,17,18,19},{20,21,22,2..., dimensions={0} | all-to-all | bytes 1048576 | tf_op jit(solution)/shard_map/all_to_all | solution.py:233
  15.2 23.2 %all_to_all.26.in_ref = f32[4,256,128]{2,1,0:T(8,128)S(1)} all-to-all(f32[4,256,128]{2,1,0:T(8,128)S(1)} %add_near.1), channel_id=1, replica_groups={{0,4,8,12},{1,5,9,13},{2,6,10,14},{3,7,11,15},{16,20,24,28},{17,21,25,2..., dimensions={0} | all-to-all | bytes 1048576 | tf_op jit(solution)/shard_map/all_to_all | solution.py:233
  38.5 9.3 %all_to_all.27 = f32[4,256,128]{2,1,0:T(8,128)S(1)} all-to-all(f32[4,256,128]{2,1,0:T(8,128)S(1)} %add_far.1), channel_id=1, replica_groups={{0,1,2,3},{4,5,6,7},{8,9,10,11},{12,13,14,15},{16,17,18,19},{20,21,22,2..., dimensions={0} | all-to-all | bytes 1048576 | tf_op jit(solution)/shard_map/all_to_all | solution.py:233
  47.8 0.0 copy-done
  47.8 0.0 copy-done.1
  47.8 0.0 copy-done.2
  47.8 0.0 copy-done.3
  47.8 5.6 %solve.1 = (f32[512,128]{1,0:T(8,128)S(1)}, f32[4,64]{1,0:T(4,128)}) custom-call(f32[16,64,128]{2,1,0:T(8,128)S(1)} %bitcast.6, f32[64,64]{1,0:T(8,128)S(1)} %copy-done.1, f32[4,64]{1,0:T(4,128)S(1)} %copy-done.2, s32[1,4]{1,0:T(1,128)S(1)} %copy-done.3, bf16[2048,768]{1,0:T(8,128)(2,1)S(1)} %copy-done), custom_call_target="tpu_custom_call" | custom-call | tf_op jit(solution)/shard_map/solve/pallas_call | solution.py:192
  53.4 26.8 %all_to_all.28.in_ref = f32[32,16,128]{2,1,0:T(8,128)S(1)} all-to-all(f32[32,16,128]{2,1,0:T(8,128)S(1)} %bitcast.9), channel_id=1, replica_groups=mesh['stu'=32,'item'=16] {'stu'}, dimensions={0} | all-to-all | bytes 524288 | tf_op jit(solution)/shard_map/all_to_all | solution.py:233
  80.3 0.1 add_stu.1
  80.3 15.4 %all_to_all.29 = f32[32,16,128]{2,1,0:T(8,128)S(1)} all-to-all(f32[32,16,128]{2,1,0:T(8,128)S(1)} %add_stu.1), channel_id=1, replica_groups=mesh['stu'=32,'item'=16] {'stu'}, dimensions={0} | all-to-all | bytes 524288 | tf_op jit(solution)/shard_map/all_to_all | solution.py:233
  95.7 0.7 finish.1
  (2 shorter events, 0.1 us)
Async XLA Ops:
  3.3 44.5 %copy-start = (bf16[2048,768]{1,0:T(8,128)(2,1)S(1)}, bf16[2048,768]{1,0:T(8,128)(2,1)}, u32[]{:S(2)}) copy-start(bf16[2048,768]{1,0:T(8,128)(2,1)} %attempts_ref.1) | copy-start | bytes 9437188
  3.3 44.5 %copy-start.1 = (f32[64,64]{1,0:T(8,128)S(1)}, f32[64,64]{1,0:T(8,128)}, u32[]{:S(2)}) copy-start(f32[64,64]{1,0:T(8,128)} %core_ref.1) | copy-start | bytes 49156
  3.3 44.5 %copy-start.2 = (f32[4,64]{1,0:T(4,128)S(1)}, f32[4,64]{1,0:T(4,128)}, u32[]{:S(2)}) copy-start(f32[4,64]{1,0:T(4,128)} %weights_ref.1) | copy-start | bytes 3076
  3.3 44.5 %copy-start.3 = (s32[1,4]{1,0:T(1,128)S(1)}, s32[1,4]{1,0:T(1,128)}, u32[]{:S(2)}) copy-start(s32[1,4]{1,0:T(1,128)} %counts_ref.1) | copy-start | bytes 52

commit v4 on v3

--- a/solution.py
+++ b/solution.py
@@ -58,23 +58,25 @@
     )(factor_t, attempts)
 
 
-def add_kernel(in_ref, out_ref):
-    total = in_ref[0]
-    for part in range(1, in_ref.shape[0]):
-        total = total + in_ref[part]
-    for part in range(out_ref.shape[0]):
-        out_ref[part] = total
-
-
-def add_and_copy(parts, copies, name):
-    return pl.pallas_call(
-        add_kernel,
+def add_kernel(in_ref, out_ref, *, parts, copies):
+    rows = in_ref.shape[0] // parts
+    total = in_ref[:rows, :]
+    for part in range(1, parts):
+        total = total + in_ref[part * rows : (part + 1) * rows, :]
+    for copy in range(copies):
+        out_ref[copy * rows : (copy + 1) * rows, :] = total
+
+
+def add_and_copy(rows, parts, copies, name):
+    out_shape = (rows.shape[0] // parts * copies, BLOCK)
+    return pl.pallas_call(
+        functools.partial(add_kernel, parts=parts, copies=copies),
         in_specs=[VMEM],
         out_specs=VMEM,
-        out_shape=jax.ShapeDtypeStruct((copies, *parts.shape[1:]), F32),
-        compiler_params=pltpu.CompilerParams(vmem_limit_bytes=2 * parts.size * 4 + 1024 * 1024),
+        out_shape=jax.ShapeDtypeStruct(out_shape, F32),
+        compiler_params=pltpu.CompilerParams(vmem_limit_bytes=2 * rows.size * 4 + 1024 * 1024),
         name=name,
-    )(parts)
+    )(rows)
 
 
 def split(value):
@@ -82,15 +84,16 @@
     return high, (value - high.astype(F32)).astype(BF16)
 
 
-def dot3(left, right_parts, dims):
+def right_factor(pair, left_lanes, right_lanes):
+    parts = [half * lanes for half in split(pair) for lanes in (left_lanes, right_lanes)]
+    return jnp.concatenate(parts, axis=0)
+
+
+def times(left, right):
     rows = left.shape[0]
-    high, low = split(left)
-    right_high, right_low = right_parts
-    both = lax.dot_general(
-        jnp.concatenate([high, low], axis=0), right_high, dims, preferred_element_type=F32
-    )
-    cross = lax.dot_general(high, right_low, dims, preferred_element_type=F32)
-    return both[:rows] + (both[rows:] + cross)
+    both = jnp.concatenate([jnp.concatenate([half, half], axis=1) for half in split(left)], axis=0)
+    product = jnp.dot(both, right, preferred_element_type=F32)
+    return product[:rows] + product[rows:]
 
 
 def solve_kernel(
@@ -111,57 +114,53 @@
         halves[block] = both
         grams[owners[block]] += lax.dot_general(both, both, NT, preferred_element_type=F32)
 
-    row_id = lax.broadcasted_iota(jnp.int32, (rank, wide), 0)
-    col_id = lax.broadcasted_iota(jnp.int32, (rank, wide), 1)
-    identity = (row_id == col_id % rank).astype(F32)
-    student_id = col_id // rank
-    on_diagonal = (
-        lax.broadcasted_iota(jnp.int32, (wide, wide), 0) // rank
-        == lax.broadcasted_iota(jnp.int32, (wide, wide), 1) // rank
-    ).astype(F32)
-
-    def diagonal(value):
-        high = value.astype(BF16).astype(F32)
-        low = value - high
-        return tuple(
-            (jnp.concatenate([half] * students, axis=0) * on_diagonal).astype(BF16)
-            for half in (high, low)
-        )
+    lane = lax.broadcasted_iota(jnp.int32, (rank, 2 * rank), 1)
+    identity = (lax.broadcasted_iota(jnp.int32, (rank, 2 * rank), 0) == lane % rank).astype(F32)
+    on_left = lane[:1] < rank
+    left_lanes = (lane < rank).astype(F32).astype(BF16)
+    right_lanes = (lane >= rank).astype(F32).astype(BF16)
+
+    def right(pair):
+        return right_factor(pair, left_lanes, right_lanes)
 
     def beside(parts):
         return jnp.concatenate(parts, axis=1)
 
     core = core_ref[...]
+    pairs = range(students // 2)
     scaled = [core * weights_ref[student : student + 1, :] for student in range(students)]
-    lift_t = beside([one.T for one in scaled])
-    lift_diagonal = diagonal(beside(scaled))
+    lift = [beside(scaled[2 * pair : 2 * pair + 2]) for pair in pairs]
+    lift_t = [beside([one.T for one in scaled[2 * pair : 2 * pair + 2]]) for pair in pairs]
+    lift_right = [right(one) for one in lift]
+    lift_t_right = [right(one) for one in lift_t]
 
     raw_grams = []
     for student in range(students):
         terms = grams[student]
         rows = terms[:rank] + terms[rank:]
         raw_grams.append(rows[:, :rank] + rows[:, rank:])
-    raw_diagonal = diagonal(beside(raw_grams))
-    gram = dot3(dot3(beside(scaled), raw_diagonal, NN), lift_diagonal, NT)
-    trace_row = jnp.sum(gram * identity, axis=0, keepdims=True)
-    inverse = jnp.zeros((1, wide), F32)
-    lane_student = student_id[:1]
-    for student in range(students):
-        here = lane_student == student
-        trace = jnp.sum(jnp.where(here, trace_row, 0.0), axis=1, keepdims=True)
-        inverse = jnp.where(here, 1.0 / jnp.sqrt(trace + 1e-06), inverse)
-    gram = gram * (inverse * inverse)
-    polynomial = lift_t * inverse
+    raw_right = [right(beside(raw_grams[2 * pair : 2 * pair + 2])) for pair in pairs]
+    gram, polynomial = [], []
+    for pair in pairs:
+        half_way = times(lift[pair], raw_right[pair])
+        row = jnp.sum(half_way * lift[pair], axis=0, keepdims=True)
+        left_trace = jnp.sum(jnp.where(on_left, row, 0.0), axis=1, keepdims=True)
+        right_trace = jnp.sum(jnp.where(on_left, 0.0, row), axis=1, keepdims=True)
+        inverse = 1.0 / jnp.sqrt(jnp.where(on_left, left_trace, right_trace) + 1e-06)
+        gram.append(times(half_way, lift_t_right[pair]) * (inverse * inverse))
+        polynomial.append(lift_t[pair] * inverse)
     for iteration in range(NS_STEPS):
-        factor_diagonal = diagonal(1.5 * identity - 0.5 * gram)
-        if iteration == NS_STEPS - 1:
-            polynomial = dot3(polynomial, factor_diagonal, NN)
-        else:
-            pair = dot3(jnp.concatenate([gram, polynomial], axis=0), factor_diagonal, NN)
-            polynomial = pair[rank:]
-            gram = dot3(pair[:rank], factor_diagonal, NN)
-
-    apply = dot3(polynomial, lift_diagonal, NN)
+        for pair in pairs:
+            factor = right(1.5 * identity - 0.5 * gram[pair])
+            if iteration == NS_STEPS - 1:
+                polynomial[pair] = times(polynomial[pair], factor)
+            else:
+                moved = times(jnp.concatenate([gram[pair], polynomial[pair]], axis=0), factor)
+                polynomial[pair] = moved[rank:]
+                gram[pair] = times(moved[:rank], factor)
+
+    apply = beside([times(polynomial[pair], lift_right[pair]) for pair in pairs])
+    polynomial = beside(polynomial)
     for student in range(students):
         high, low = split(apply[:, student * rank : (student + 1) * rank])
         lifts[student] = jnp.concatenate([beside([high, high]), beside([low, low])], axis=0)
@@ -172,7 +171,7 @@
     item_part = jnp.dot(beside(weighted), attempts_ref[...], preferred_element_type=F32)
 
     turned = beside([polynomial[:, k * rank : (k + 1) * rank].T for k in range(students)])
-    crossed = dot3(turned, raw_diagonal, NN)
+    crossed = beside([times(turned[:, 2 * pair * rank : 2 * (pair + 1) * rank], raw_right[pair]) for pair in pairs])
     shared = jnp.zeros((rank, rank), F32)
     for student in range(students):
         one = crossed[:, student * rank : (student + 1) * rank]
@@ -182,8 +181,8 @@
     tiles = item_part.shape[1] // BLOCK
     for tile in range(tiles):
         parts_ref[tile * rank : (tile + 1) * rank, :] = item_part[:, tile * BLOCK : (tile + 1) * BLOCK]
-    parts_ref[tiles * rank :, :] = jnp.zeros((parts_ref.shape[0] - tiles * rank, BLOCK), F32)
-    parts_ref[tiles * rank : (tiles + 1) * rank, :rank] = shared
+    last = tiles * rank
+    parts_ref[last : last + rank // 2, :] = beside([shared[: rank // 2], shared[rank // 2 :]])
 
 
 def solve(raw, core_factor, student_weights, blocks, attempts, part_rows):
@@ -212,7 +211,9 @@
     for tile in range(items // BLOCK):
         item_ref[:, tile * BLOCK : (tile + 1) * BLOCK] = total_ref[tile * rank : (tile + 1) * rank, :]
     last = items // BLOCK * rank
-    shared_ref[...] = total_ref[last : last + rank, :rank]
+    both = total_ref[last : last + rank // 2, :]
+    shared_ref[: rank // 2, :] = both[:, :rank]
+    shared_ref[rank // 2 :, :] = both[:, rank:]
 
 
 def finish(total, rank, items):
@@ -229,30 +230,32 @@
     )(total)
 
 
-def exchange(parts, axis, groups=None):
-    return lax.all_to_all(parts, axis, 0, 0, tiled=True, axis_index_groups=groups)
-
-
-def sum_over_item(parts, n_item):
-    near = [[far * NEAR + i for i in range(NEAR)] for far in range(n_item // NEAR)]
-    distant = [[far * NEAR + i for far in range(n_item // NEAR)] for i in range(NEAR)]
-    shares = parts.reshape(NEAR, -1, BLOCK)
-    shares = exchange(shares, "item", near)
-    shares = exchange(add_and_copy(shares, n_item // NEAR, "add_near"), "item", distant)
-    shares = exchange(add_and_copy(shares, NEAR, "add_far"), "item", near)
-    return shares.reshape(parts.shape)
+def exchange(rows, parts, axis, groups=None):
+    parted = rows.reshape(parts, -1, 1, BLOCK)
+    return lax.all_to_all(parted, axis, 0, 0, tiled=True, axis_index_groups=groups).reshape(rows.shape)
+
+
+def sum_over_item(rows, n_item):
+    n_far = n_item // NEAR
+    near = [[far * NEAR + i for i in range(NEAR)] for far in range(n_far)]
+    distant = [[far * NEAR + i for far in range(n_far)] for i in range(NEAR)]
+    rows = exchange(rows, NEAR, "item", near)
+    rows = exchange(add_and_copy(rows, NEAR, n_far, "add_near"), n_far, "item", distant)
+    return exchange(add_and_copy(rows, n_far, NEAR, "add_far"), NEAR, "item", near)
+
+
+def sum_over_stu(rows, n_stu):
+    rows = exchange(rows, n_stu, "stu")
+    return exchange(add_and_copy(rows, n_stu, n_stu, "add_stu"), n_stu, "stu")
 
 
 def local(n_stu, n_item, attempts, item_factor, core_factor, student_weights, blocks):
     items, rank = item_factor.shape
-    raw = sum_over_item(project(attempts, item_factor.T, 2), n_item)
-    tiles = items // BLOCK
-    step = 8 * n_stu
-    part_rows = -(-(tiles + 1) * rank // step) * step
-    parts, student_part = solve(raw, core_factor, student_weights, blocks, attempts, part_rows)
-    parts = exchange(parts.reshape(n_stu, part_rows // n_stu, BLOCK), "stu")
-    total = exchange(add_and_copy(parts, n_stu, "add_stu"), "stu").reshape(part_rows, BLOCK)
-    item_total, shared_total = finish(total, rank, items)
+    sums = project(attempts, item_factor.T, 2)
+    raw = sum_over_item(sums.reshape(-1, BLOCK), n_item).reshape(sums.shape)
+    used = items // BLOCK * rank + rank // 2
+    parts, student_part = solve(raw, core_factor, student_weights, blocks, attempts, -(-used // n_stu) * n_stu)
+    item_total, shared_total = finish(sum_over_stu(parts, n_stu), rank, items)
     return (item_total.T, shared_total, student_part)
 
 

time: 96.7 us -> 94.7 us (0.979)
  blocking collectives: 86.6 us -> 84.7 us
    all_to_all x5, blocking collectives: 86.6 us -> 84.7 us  [exchange(): lax.all_to_all(parted, axis, 0, 0, tiled=True, axis_index_groups=groups)]
where the time goes in v4:
time: 94.7 us; the launch traced here: 94.4 us
  blocking collectives  84.7 us (89%)
  Pallas kernels  8.91 us (9%)
    all_to_all x5, blocking collectives, exchange(): lax.all_to_all(parted, axis, 0, 0, tiled=True, axis_index_groups=groups)  84.7 us
    pallas_call x1, Pallas kernels, solve(): pl.pallas_call(solve_kernel, in_specs=[VMEM, VMEM, VMEM, SMEM, VMEM], out...  5.45 us
    pallas_call x1, Pallas kernels, project(): pl.pallas_call(project_kernel, in_specs=[pl.BlockSpec(memory_space=pl.ANY...  2.63 us

profile of v4, /device:TPU:1, one launch (start us, length us, event | category | flops | bytes accessed | tf_op | source)
XLA Modules:
  0.0 94.4 jit_solution(8049604511432643962)
XLA Ops:
  0.6 2.6 %project.1 = f32[16,64,128]{2,1,0:T(8,128)S(1)} custom-call(bf16[64,768]{1,0:T(8,128)(2,1)} %bitcast.28, bf16[2048,768]{1,0:T(8,128)(2,1)} %attempts_ref.1), custom_call_target="tpu_custom_call" | custom-call | tf_op jit(solution)/shard_map/project/pallas_call | solution.py:45
  3.3 0.0 copy-start
  3.3 0.0 copy-start.1
  3.3 0.0 copy-start.2
  3.3 0.0 copy-start.3
  3.3 11.8 %all_to_all.25 = f32[4,256,1,128]{3,1,2,0:T(8,128)S(1)} all-to-all(f32[4,256,1,128]{3,1,2,0:T(8,128)S(1)} %bitcast.19), channel_id=1, replica_groups={{0,1,2,3},{4,5,6,7},{8,9,10,11},{12,13,14,15},{16,17,18,19},{20,21,22,2..., dimensions={0} | all-to-all | bytes 1048576 | tf_op jit(solution)/shard_map/all_to_all | solution.py:235
  15.2 23.2 %all_to_all.26 = f32[4,256,1,128]{3,1,2,0:T(8,128)S(1)} all-to-all(f32[4,256,1,128]{3,1,2,0:T(8,128)S(1)} %bitcast.21), channel_id=1, replica_groups={{0,4,8,12},{1,5,9,13},{2,6,10,14},{3,7,11,15},{16,20,24,28},{17,21,25,2..., dimensions={0} | all-to-all | bytes 1048576 | tf_op jit(solution)/shard_map/all_to_all | solution.py:235
  38.5 9.3 %all_to_all.27 = f32[4,256,1,128]{3,1,2,0:T(8,128)S(1)} all-to-all(f32[4,256,1,128]{3,1,2,0:T(8,128)S(1)} %bitcast.23), channel_id=1, replica_groups={{0,1,2,3},{4,5,6,7},{8,9,10,11},{12,13,14,15},{16,17,18,19},{20,21,22,2..., dimensions={0} | all-to-all | bytes 1048576 | tf_op jit(solution)/shard_map/all_to_all | solution.py:235
  47.8 0.0 copy-done
  47.8 0.0 copy-done.1
  47.8 0.0 copy-done.2
  47.8 0.0 copy-done.3
  47.8 5.5 %solve.1 = (f32[416,128]{1,0:T(8,128)S(1)}, f32[4,64]{1,0:T(4,128)}) custom-call(f32[16,64,128]{2,1,0:T(8,128)S(1)} %bitcast.18, f32[64,64]{1,0:T(8,128)S(1)} %copy-done.1, f32[4,64]{1,0:T(4,128)S(1)} %copy-done.2, s32[1,4]{1,0:T(1,128)S(1)} %copy-done.3, bf16[2048,768]{1,0:T(8,128)(2,1)S(1)} %copy-done), custom_call_target="tpu_custom_call" | custom-call | tf_op jit(solution)/shard_map/solve/pallas_call | solution.py:191
  53.3 26.0 %all_to_all.28 = f32[32,13,1,128]{3,2,1,0:T(1,128)S(1)} all-to-all(f32[32,13,1,128]{3,2,1,0:T(1,128)S(1)} %bitcast.27), channel_id=1, replica_groups=mesh['stu'=32,'item'=16] {'stu'}, dimensions={0} | all-to-all | bytes 425984 | tf_op jit(solution)/shard_map/all_to_all | solution.py:235
  79.3 0.1 add_stu.1
  79.4 14.3 %all_to_all.29 = f32[32,13,1,128]{3,2,1,0:T(1,128)S(1)} all-to-all(f32[32,13,1,128]{3,2,1,0:T(1,128)S(1)} %bitcast.26), channel_id=1, replica_groups=mesh['stu'=32,'item'=16] {'stu'}, dimensions={0} | all-to-all | bytes 425984 | tf_op jit(solution)/shard_map/all_to_all | solution.py:235
  93.7 0.7 finish.1
  (2 shorter events, 0.1 us)
Async XLA Ops:
  3.3 44.5 %copy-start = (bf16[2048,768]{1,0:T(8,128)(2,1)S(1)}, bf16[2048,768]{1,0:T(8,128)(2,1)}, u32[]{:S(2)}) copy-start(bf16[2048,768]{1,0:T(8,128)(2,1)} %attempts_ref.1) | copy-start | bytes 9437188
  3.3 44.5 %copy-start.1 = (f32[64,64]{1,0:T(8,128)S(1)}, f32[64,64]{1,0:T(8,128)}, u32[]{:S(2)}) copy-start(f32[64,64]{1,0:T(8,128)} %core_ref.1) | copy-start | bytes 49156
  3.3 44.5 %copy-start.2 = (f32[4,64]{1,0:T(4,128)S(1)}, f32[4,64]{1,0:T(4,128)}, u32[]{:S(2)}) copy-start(f32[4,64]{1,0:T(4,128)} %weights_ref.1) | copy-start | bytes 3076
  3.3 44.5 %copy-start.3 = (s32[1,4]{1,0:T(1,128)S(1)}, s32[1,4]{1,0:T(1,128)}, u32[]{:S(2)}) copy-start(s32[1,4]{1,0:T(1,128)} %counts_ref.1) | copy-start | bytes 52

commit v5 on v4

--- a/solution.py
+++ b/solution.py
@@ -11,6 +11,7 @@
 PROJECT_VMEM = 56 * 1024 * 1024
 BLOCK = 128
 NEAR = 4
+RING = (0, 1, 3, 2)
 F32 = jnp.float32
 BF16 = jnp.bfloat16
 NN = (((1,), (0,)), ((), ()))
@@ -150,14 +151,11 @@
         gram.append(times(half_way, lift_t_right[pair]) * (inverse * inverse))
         polynomial.append(lift_t[pair] * inverse)
     for iteration in range(NS_STEPS):
-        for pair in pairs:
-            factor = right(1.5 * identity - 0.5 * gram[pair])
-            if iteration == NS_STEPS - 1:
-                polynomial[pair] = times(polynomial[pair], factor)
-            else:
-                moved = times(jnp.concatenate([gram[pair], polynomial[pair]], axis=0), factor)
-                polynomial[pair] = moved[rank:]
-                gram[pair] = times(moved[:rank], factor)
+        factor = [right(1.5 * identity - 0.5 * gram[pair]) for pair in pairs]
+        if iteration < NS_STEPS - 1:
+            moved = [times(gram[pair], factor[pair]) for pair in pairs]
+            gram = [times(moved[pair], factor[pair]) for pair in pairs]
+        polynomial = [times(polynomial[pair], factor[pair]) for pair in pairs]
 
     apply = beside([times(polynomial[pair], lift_right[pair]) for pair in pairs])
     polynomial = beside(polynomial)
@@ -235,10 +233,10 @@
     return lax.all_to_all(parted, axis, 0, 0, tiled=True, axis_index_groups=groups).reshape(rows.shape)
 
 
-def sum_over_item(rows, n_item):
-    n_far = n_item // NEAR
-    near = [[far * NEAR + i for i in range(NEAR)] for far in range(n_far)]
-    distant = [[far * NEAR + i for far in range(n_far)] for i in range(NEAR)]
+def sum_over_item(rows):
+    n_far = len(RING)
+    near = [[far * NEAR + i for i in RING] for far in range(n_far)]
+    distant = [[far * NEAR + i for far in RING] for i in range(NEAR)]
     rows = exchange(rows, NEAR, "item", near)
     rows = exchange(add_and_copy(rows, NEAR, n_far, "add_near"), n_far, "item", distant)
     return exchange(add_and_copy(rows, n_far, NEAR, "add_far"), NEAR, "item", near)
@@ -249,10 +247,10 @@
     return exchange(add_and_copy(rows, n_stu, n_stu, "add_stu"), n_stu, "stu")
 
 
-def local(n_stu, n_item, attempts, item_factor, core_factor, student_weights, blocks):
+def local(n_stu, attempts, item_factor, core_factor, student_weights, blocks):
     items, rank = item_factor.shape
     sums = project(attempts, item_factor.T, 2)
-    raw = sum_over_item(sums.reshape(-1, BLOCK), n_item).reshape(sums.shape)
+    raw = sum_over_item(sums.reshape(-1, BLOCK)).reshape(sums.shape)
     used = items // BLOCK * rank + rank // 2
     parts, student_part = solve(raw, core_factor, student_weights, blocks, attempts, -(-used // n_stu) * n_stu)
     item_total, shared_total = finish(sum_over_stu(parts, n_stu), rank, items)
@@ -262,5 +260,5 @@
 def solution(mesh):
     in_specs = (P("stu", "item"), P("item", None), P(), P("stu", None), P("stu", None))
     out_specs = (P("item", None), P(), P("stu", None))
-    body = functools.partial(local, mesh.shape["stu"], mesh.shape["item"])
+    body = functools.partial(local, mesh.shape["stu"])
     return jax.shard_map(body, mesh=mesh, in_specs=in_specs, out_specs=out_specs, check_vma=False)

time: 94.7 us -> 94.1 us (level)
  no operation moved by 1% of the time
where the time goes in v5:
time: 94.1 us; the launch traced here: 93.8 us
  blocking collectives  84.5 us (90%)
  Pallas kernels  8.61 us (9%)
    all_to_all x5, blocking collectives, exchange(): lax.all_to_all(parted, axis, 0, 0, tiled=True, axis_index_groups=groups)  84.5 us
    pallas_call x1, Pallas kernels, solve(): pl.pallas_call(solve_kernel, in_specs=[VMEM, VMEM, VMEM, SMEM, VMEM], out...  5.15 us
    pallas_call x1, Pallas kernels, project(): pl.pallas_call(project_kernel, in_specs=[pl.BlockSpec(memory_space=pl.ANY...  2.63 us

profile of v5, /device:TPU:1, one launch (start us, length us, event | category | flops | bytes accessed | tf_op | source)
XLA Modules:
  0.0 93.8 jit_solution(13459876180699277916)
XLA Ops:
  0.6 2.6 %project.1 = f32[16,64,128]{2,1,0:T(8,128)S(1)} custom-call(bf16[64,768]{1,0:T(8,128)(2,1)} %bitcast.28, bf16[2048,768]{1,0:T(8,128)(2,1)} %attempts_ref.1), custom_call_target="tpu_custom_call" | custom-call | tf_op jit(solution)/shard_map/project/pallas_call | solution.py:46
  3.3 0.0 copy-start
  3.3 0.0 copy-start.1
  3.3 0.0 copy-start.2
  3.3 0.0 copy-start.3
  3.3 11.5 %all_to_all.25 = f32[4,256,1,128]{3,1,2,0:T(8,128)S(1)} all-to-all(f32[4,256,1,128]{3,1,2,0:T(8,128)S(1)} %bitcast.19), channel_id=1, replica_groups={{0,1,3,2},{4,5,7,6},{8,9,11,10},{12,13,15,14},{16,17,19,18},{20,21,23,2..., dimensions={0} | all-to-all | bytes 1048576 | tf_op jit(solution)/shard_map/all_to_all | solution.py:233
  14.9 22.5 %all_to_all.26 = f32[4,256,1,128]{3,1,2,0:T(8,128)S(1)} all-to-all(f32[4,256,1,128]{3,1,2,0:T(8,128)S(1)} %bitcast.21), channel_id=1, replica_groups={{0,4,12,8},{1,5,13,9},{2,6,14,10},{3,7,15,11},{16,20,28,24},{17,21,29,2..., dimensions={0} | all-to-all | bytes 1048576 | tf_op jit(solution)/shard_map/all_to_all | solution.py:233
  37.5 9.0 %all_to_all.27 = f32[4,256,1,128]{3,1,2,0:T(8,128)S(1)} all-to-all(f32[4,256,1,128]{3,1,2,0:T(8,128)S(1)} %bitcast.23), channel_id=1, replica_groups={{0,1,3,2},{4,5,7,6},{8,9,11,10},{12,13,15,14},{16,17,19,18},{20,21,23,2..., dimensions={0} | all-to-all | bytes 1048576 | tf_op jit(solution)/shard_map/all_to_all | solution.py:233
  46.5 0.0 copy-done
  46.5 0.0 copy-done.1
  46.5 0.0 copy-done.2
  46.5 0.0 copy-done.3
  46.5 5.2 %solve.1 = (f32[416,128]{1,0:T(8,128)S(1)}, f32[4,64]{1,0:T(4,128)}) custom-call(f32[16,64,128]{2,1,0:T(8,128)S(1)} %bitcast.18, f32[64,64]{1,0:T(8,128)S(1)} %copy-done.1, f32[4,64]{1,0:T(4,128)S(1)} %copy-done.2, s32[1,4]{1,0:T(1,128)S(1)} %copy-done.3, bf16[2048,768]{1,0:T(8,128)(2,1)S(1)} %copy-done), custom_call_target="tpu_custom_call" | custom-call | tf_op jit(solution)/shard_map/solve/pallas_call | solution.py:189
  51.7 27.0 %all_to_all.28 = f32[32,13,1,128]{3,2,1,0:T(1,128)S(1)} all-to-all(f32[32,13,1,128]{3,2,1,0:T(1,128)S(1)} %bitcast.27), channel_id=1, replica_groups=mesh['stu'=32,'item'=16] {'stu'}, dimensions={0} | all-to-all | bytes 425984 | tf_op jit(solution)/shard_map/all_to_all | solution.py:233
  78.7 0.1 add_stu.1
  78.8 14.3 %all_to_all.29 = f32[32,13,1,128]{3,2,1,0:T(1,128)S(1)} all-to-all(f32[32,13,1,128]{3,2,1,0:T(1,128)S(1)} %bitcast.26), channel_id=1, replica_groups=mesh['stu'=32,'item'=16] {'stu'}, dimensions={0} | all-to-all | bytes 425984 | tf_op jit(solution)/shard_map/all_to_all | solution.py:233
  93.1 0.7 finish.1
  (2 shorter events, 0.1 us)
Async XLA Ops:
  3.3 43.2 %copy-start = (bf16[2048,768]{1,0:T(8,128)(2,1)S(1)}, bf16[2048,768]{1,0:T(8,128)(2,1)}, u32[]{:S(2)}) copy-start(bf16[2048,768]{1,0:T(8,128)(2,1)} %attempts_ref.1) | copy-start | bytes 9437188
  3.3 43.2 %copy-start.1 = (f32[64,64]{1,0:T(8,128)S(1)}, f32[64,64]{1,0:T(8,128)}, u32[]{:S(2)}) copy-start(f32[64,64]{1,0:T(8,128)} %core_ref.1) | copy-start | bytes 49156
  3.3 43.2 %copy-start.2 = (f32[4,64]{1,0:T(4,128)S(1)}, f32[4,64]{1,0:T(4,128)}, u32[]{:S(2)}) copy-start(f32[4,64]{1,0:T(4,128)} %weights_ref.1) | copy-start | bytes 3076
  3.3 43.2 %copy-start.3 = (s32[1,4]{1,0:T(1,128)S(1)}, s32[1,4]{1,0:T(1,128)}, u32[]{:S(2)}) copy-start(s32[1,4]{1,0:T(1,128)} %counts_ref.1) | copy-start | bytes 52

commit v6 on v5

--- a/solution.py
+++ b/solution.py
@@ -10,7 +10,8 @@
 NS_STEPS = 6
 PROJECT_VMEM = 56 * 1024 * 1024
 BLOCK = 128
-NEAR = 4
+NEAR_ITEM = 4
+NEAR_STU = 8
 RING = (0, 1, 3, 2)
 F32 = jnp.float32
 BF16 = jnp.bfloat16
@@ -233,27 +234,22 @@
     return lax.all_to_all(parted, axis, 0, 0, tiled=True, axis_index_groups=groups).reshape(rows.shape)
 
 
-def sum_over_item(rows):
+def sum_over(axis, n_near, rows):
     n_far = len(RING)
-    near = [[far * NEAR + i for i in RING] for far in range(n_far)]
-    distant = [[far * NEAR + i for far in RING] for i in range(NEAR)]
-    rows = exchange(rows, NEAR, "item", near)
-    rows = exchange(add_and_copy(rows, NEAR, n_far, "add_near"), n_far, "item", distant)
-    return exchange(add_and_copy(rows, n_far, NEAR, "add_far"), NEAR, "item", near)
-
-
-def sum_over_stu(rows, n_stu):
-    rows = exchange(rows, n_stu, "stu")
-    return exchange(add_and_copy(rows, n_stu, n_stu, "add_stu"), n_stu, "stu")
+    near = [[far * n_near + i for i in range(n_near)] for far in range(n_far)]
+    distant = [[far * n_near + i for far in RING] for i in range(n_near)]
+    rows = exchange(rows, n_near, axis, near)
+    rows = exchange(add_and_copy(rows, n_near, n_far, "add_near_" + axis), n_far, axis, distant)
+    return exchange(add_and_copy(rows, n_far, n_near, "add_far_" + axis), n_near, axis, near)
 
 
 def local(n_stu, attempts, item_factor, core_factor, student_weights, blocks):
     items, rank = item_factor.shape
     sums = project(attempts, item_factor.T, 2)
-    raw = sum_over_item(sums.reshape(-1, BLOCK)).reshape(sums.shape)
+    raw = sum_over("item", NEAR_ITEM, sums.reshape(-1, BLOCK)).reshape(sums.shape)
     used = items // BLOCK * rank + rank // 2
     parts, student_part = solve(raw, core_factor, student_weights, blocks, attempts, -(-used // n_stu) * n_stu)
-    item_total, shared_total = finish(sum_over_stu(parts, n_stu), rank, items)
+    item_total, shared_total = finish(sum_over("stu", NEAR_STU, parts), rank, items)
     return (item_total.T, shared_total, student_part)
 
 

time: 94.1 us -> 92.6 us (0.984)
  blocking collectives: 84.5 us -> 83 us
    all_to_all x5 -> x6, blocking collectives: 84.5 us -> 83 us  [exchange(): lax.all_to_all(parted, axis, 0, 0, tiled=True, axis_index_groups=groups)]
where the time goes in v6:
time: 92.6 us; the launch traced here: 92.3 us
  blocking collectives  83 us (90%)
  Pallas kernels  8.61 us (9%)
    all_to_all x6, blocking collectives, exchange(): lax.all_to_all(parted, axis, 0, 0, tiled=True, axis_index_groups=groups)  83 us
    pallas_call x1, Pallas kernels, solve(): pl.pallas_call(solve_kernel, in_specs=[VMEM, VMEM, VMEM, SMEM, VMEM], out...  5.17 us
    pallas_call x1, Pallas kernels, project(): pl.pallas_call(project_kernel, in_specs=[pl.BlockSpec(memory_space=pl.ANY...  2.63 us

profile of v6, /device:TPU:1, one launch (start us, length us, event | category | flops | bytes accessed | tf_op | source)
XLA Modules:
  0.0 92.3 jit_solution(2706121118268127569)
XLA Ops:
  0.6 2.6 %project.1 = f32[16,64,128]{2,1,0:T(8,128)S(1)} custom-call(bf16[64,768]{1,0:T(8,128)(2,1)} %bitcast.32, bf16[2048,768]{1,0:T(8,128)(2,1)} %attempts_ref.1), custom_call_target="tpu_custom_call" | custom-call | tf_op jit(solution)/shard_map/project/pallas_call | solution.py:47
  3.3 0.0 copy-start
  3.3 0.0 copy-start.1
  3.3 0.0 copy-start.2
  3.3 0.0 copy-start.3
  3.3 11.8 %all_to_all.30 = f32[4,256,1,128]{3,1,2,0:T(8,128)S(1)} all-to-all(f32[4,256,1,128]{3,1,2,0:T(8,128)S(1)} %bitcast.21), channel_id=1, replica_groups={{0,1,2,3},{4,5,6,7},{8,9,10,11},{12,13,14,15},{16,17,18,19},{20,21,22,2..., dimensions={0} | all-to-all | bytes 1048576 | tf_op jit(solution)/shard_map/all_to_all | solution.py:234
  15.2 22.5 %all_to_all.31 = f32[4,256,1,128]{3,1,2,0:T(8,128)S(1)} all-to-all(f32[4,256,1,128]{3,1,2,0:T(8,128)S(1)} %bitcast.23), channel_id=1, replica_groups={{0,4,12,8},{1,5,13,9},{2,6,14,10},{3,7,15,11},{16,20,28,24},{17,21,29,2..., dimensions={0} | all-to-all | bytes 1048576 | tf_op jit(solution)/shard_map/all_to_all | solution.py:234
  37.8 9.3 %all_to_all.32 = f32[4,256,1,128]{3,1,2,0:T(8,128)S(1)} all-to-all(f32[4,256,1,128]{3,1,2,0:T(8,128)S(1)} %bitcast.25), channel_id=1, replica_groups={{0,1,2,3},{4,5,6,7},{8,9,10,11},{12,13,14,15},{16,17,18,19},{20,21,22,2..., dimensions={0} | all-to-all | bytes 1048576 | tf_op jit(solution)/shard_map/all_to_all | solution.py:234
  47.1 0.0 copy-done
  47.1 0.0 copy-done.1
  47.1 0.0 copy-done.2
  47.1 0.0 copy-done.3
  47.1 5.2 %solve.1 = (f32[416,128]{1,0:T(8,128)S(1)}, f32[4,64]{1,0:T(4,128)}) custom-call(f32[16,64,128]{2,1,0:T(8,128)S(1)} %bitcast.20, f32[64,64]{1,0:T(8,128)S(1)} %copy-done.1, f32[4,64]{1,0:T(4,128)S(1)} %copy-done.2, s32[1,4]{1,0:T(1,128)S(1)} %copy-done.3, bf16[2048,768]{1,0:T(8,128)(2,1)S(1)} %copy-done), custom_call_target="tpu_custom_call" | custom-call | tf_op jit(solution)/shard_map/solve/pallas_call | solution.py:190
  52.3 16.8 %all_to_all.33 = f32[8,52,1,128]{3,2,1,0:T(1,128)S(1)} all-to-all(f32[8,52,1,128]{3,2,1,0:T(1,128)S(1)} %bitcast.31), channel_id=1, replica_groups={{0,16,32,48,64,80,96,112},{128,144,160,176,192,208,224,240},{256,272,28..., dimensions={0} | all-to-all | bytes 425984 | tf_op jit(solution)/shard_map/all_to_all | solution.py:234
  69.1 12.9 %all_to_all.34 = f32[4,52,1,128]{3,2,1,0:T(1,128)S(1)} all-to-all(f32[4,52,1,128]{3,2,1,0:T(1,128)S(1)} %bitcast.29), channel_id=1, replica_groups={{0,128,384,256},{16,144,400,272},{32,160,416,288},{48,176,432,304},{64,..., dimensions={0} | all-to-all | bytes 212992 | tf_op jit(solution)/shard_map/all_to_all | solution.py:234
  82.0 9.6 %all_to_all.35 = f32[8,52,1,128]{3,2,1,0:T(1,128)S(1)} all-to-all(f32[8,52,1,128]{3,2,1,0:T(1,128)S(1)} %bitcast.27), channel_id=1, replica_groups={{0,16,32,48,64,80,96,112},{128,144,160,176,192,208,224,240},{256,272,28..., dimensions={0} | all-to-all | bytes 425984 | tf_op jit(solution)/shard_map/all_to_all | solution.py:234
  91.6 0.7 finish.1
  (4 shorter events, 0.1 us)
Async XLA Ops:
  3.3 43.8 %copy-start = (bf16[2048,768]{1,0:T(8,128)(2,1)S(1)}, bf16[2048,768]{1,0:T(8,128)(2,1)}, u32[]{:S(2)}) copy-start(bf16[2048,768]{1,0:T(8,128)(2,1)} %attempts_ref.1) | copy-start | bytes 9437188
  3.3 43.8 %copy-start.1 = (f32[64,64]{1,0:T(8,128)S(1)}, f32[64,64]{1,0:T(8,128)}, u32[]{:S(2)}) copy-start(f32[64,64]{1,0:T(8,128)} %core_ref.1) | copy-start | bytes 49156
  3.3 43.8 %copy-start.2 = (f32[4,64]{1,0:T(4,128)S(1)}, f32[4,64]{1,0:T(4,128)}, u32[]{:S(2)}) copy-start(f32[4,64]{1,0:T(4,128)} %weights_ref.1) | copy-start | bytes 3076
  3.3 43.8 %copy-start.3 = (s32[1,4]{1,0:T(1,128)S(1)}, s32[1,4]{1,0:T(1,128)}, u32[]{:S(2)}) copy-start(s32[1,4]{1,0:T(1,128)} %counts_ref.1) | copy-start | bytes 52

commit v7 on v6

--- a/solution.py
+++ b/solution.py
@@ -1,4 +1,5 @@
 import functools
+import math
 
 import jax
 import jax.numpy as jnp
@@ -12,7 +13,7 @@
 BLOCK = 128
 NEAR_ITEM = 4
 NEAR_STU = 8
-RING = (0, 1, 3, 2)
+RING = (0, 1, 2, 3)
 F32 = jnp.float32
 BF16 = jnp.bfloat16
 NN = (((1,), (0,)), ((), ()))
@@ -76,7 +77,7 @@
         in_specs=[VMEM],
         out_specs=VMEM,
         out_shape=jax.ShapeDtypeStruct(out_shape, F32),
-        compiler_params=pltpu.CompilerParams(vmem_limit_bytes=2 * rows.size * 4 + 1024 * 1024),
+        compiler_params=pltpu.CompilerParams(vmem_limit_bytes=max(rows.size, math.prod(out_shape)) * 8 + 1024 * 1024),
         name=name,
     )(rows)
 
@@ -234,22 +235,26 @@
     return lax.all_to_all(parted, axis, 0, 0, tiled=True, axis_index_groups=groups).reshape(rows.shape)
 
 
-def sum_over(axis, n_near, rows):
+def sum_over(axis, n_near, rows, gather):
     n_far = len(RING)
     near = [[far * n_near + i for i in range(n_near)] for far in range(n_far)]
     distant = [[far * n_near + i for far in RING] for i in range(n_near)]
     rows = exchange(rows, n_near, axis, near)
-    rows = exchange(add_and_copy(rows, n_near, n_far, "add_near_" + axis), n_far, axis, distant)
+    if gather:
+        share = add_and_copy(rows, n_near, 1, "add_near_" + axis)
+        rows = lax.all_gather(share, axis, axis_index_groups=distant, tiled=True)
+    else:
+        rows = exchange(add_and_copy(rows, n_near, n_far, "add_near_" + axis), n_far, axis, distant)
     return exchange(add_and_copy(rows, n_far, n_near, "add_far_" + axis), n_near, axis, near)
 
 
 def local(n_stu, attempts, item_factor, core_factor, student_weights, blocks):
     items, rank = item_factor.shape
     sums = project(attempts, item_factor.T, 2)
-    raw = sum_over("item", NEAR_ITEM, sums.reshape(-1, BLOCK)).reshape(sums.shape)
+    raw = sum_over("item", NEAR_ITEM, sums.reshape(-1, BLOCK), True).reshape(sums.shape)
     used = items // BLOCK * rank + rank // 2
     parts, student_part = solve(raw, core_factor, student_weights, blocks, attempts, -(-used // n_stu) * n_stu)
-    item_total, shared_total = finish(sum_over("stu", NEAR_STU, parts), rank, items)
+    item_total, shared_total = finish(sum_over("stu", NEAR_STU, parts, False), rank, items)
     return (item_total.T, shared_total, student_part)
 
 

time: 92.6 us -> 89.1 us (0.962)
  blocking collectives: 83 us -> 79.5 us
    all_to_all x6 -> x5, blocking collectives: 83 us -> 58.2 us  [exchange(): lax.all_to_all(parted, axis, 0, 0, tiled=True, axis_index_groups=groups)]
    all_gather x0 -> x1, blocking collectives: none -> 21.2 us  [sum_over(): rows = lax.all_gather(share, axis, axis_index_groups=distant, tiled=True)]
where the time goes in v7:
time: 89.1 us; the launch traced here: 88.8 us
  blocking collectives  79.5 us (89%)
  Pallas kernels  8.59 us (10%)
    all_to_all x5, blocking collectives, exchange(): lax.all_to_all(parted, axis, 0, 0, tiled=True, axis_index_groups=groups)  58.2 us
    all_gather x1, blocking collectives, sum_over(): rows = lax.all_gather(share, axis, axis_index_groups=distant, tiled=True)  21.2 us
    pallas_call x1, Pallas kernels, solve(): pl.pallas_call(solve_kernel, in_specs=[VMEM, VMEM, VMEM, SMEM, VMEM], out...  5.16 us
    pallas_call x1, Pallas kernels, project(): pl.pallas_call(project_kernel, in_specs=[pl.BlockSpec(memory_space=pl.ANY...  2.63 us

profile of v7, /device:TPU:1, one launch (start us, length us, event | category | flops | bytes accessed | tf_op | source)
XLA Modules:
  0.0 88.8 jit_solution(18052534774389293866)
XLA Ops:
  0.6 2.6 %project.1 = f32[16,64,128]{2,1,0:T(8,128)S(1)} custom-call(bf16[64,768]{1,0:T(8,128)(2,1)} %bitcast.26, bf16[2048,768]{1,0:T(8,128)(2,1)} %attempts_ref.1), custom_call_target="tpu_custom_call" | custom-call | tf_op jit(solution)/shard_map/project/pallas_call | solution.py:48
  3.3 0.0 copy-start
  3.3 0.0 copy-start.1
  3.3 0.0 copy-start.2
  3.3 0.0 copy-start.3
  3.3 11.8 %all_to_all.25 = f32[4,256,1,128]{3,1,2,0:T(8,128)S(1)} all-to-all(f32[4,256,1,128]{3,1,2,0:T(8,128)S(1)} %bitcast.17), channel_id=1, replica_groups={{0,1,2,3},{4,5,6,7},{8,9,10,11},{12,13,14,15},{16,17,18,19},{20,21,22,2..., dimensions={0} | all-to-all | bytes 1048576 | tf_op jit(solution)/shard_map/all_to_all | solution.py:235
  15.2 21.2 %all_gather.3.in_ref = f32[1024,128]{1,0:T(8,128)S(1)} all-gather(f32[256,128]{1,0:T(8,128)S(1)} %add_near_item.1), channel_id=1, replica_groups={{0,4,8,12},{1,5,9,13},{2,6,10,14},{3,7,11,15},{16,20,24,28},{17,21,25,2..., dimensions={0}, use_global_device_ids=true | all-gather | bytes 655360 | tf_op jit(solution)/shard_map/all_gather | solution.py:245
  36.5 9.3 %all_to_all.26 = f32[4,256,1,128]{3,1,2,0:T(8,128)S(1)} all-to-all(f32[4,256,1,128]{3,1,2,0:T(8,128)S(1)} %bitcast.19), channel_id=1, replica_groups={{0,1,2,3},{4,5,6,7},{8,9,10,11},{12,13,14,15},{16,17,18,19},{20,21,22,2..., dimensions={0} | all-to-all | bytes 1048576 | tf_op jit(solution)/shard_map/all_to_all | solution.py:235
  45.8 0.0 copy-done
  45.8 0.0 copy-done.1
  45.8 0.0 copy-done.2
  45.8 0.0 copy-done.3
  45.8 5.2 %solve.1 = (f32[416,128]{1,0:T(8,128)S(1)}, f32[4,64]{1,0:T(4,128)}) custom-call(f32[16,64,128]{2,1,0:T(8,128)S(1)} %bitcast.16, f32[64,64]{1,0:T(8,128)S(1)} %copy-done.1, f32[4,64]{1,0:T(4,128)S(1)} %copy-done.2, s32[1,4]{1,0:T(1,128)S(1)} %copy-done.3, bf16[2048,768]{1,0:T(8,128)(2,1)S(1)} %copy-done), custom_call_target="tpu_custom_call" | custom-call | tf_op jit(solution)/shard_map/solve/pallas_call | solution.py:191
  51.0 13.9 %all_to_all.27 = f32[8,52,1,128]{3,2,1,0:T(1,128)S(1)} all-to-all(f32[8,52,1,128]{3,2,1,0:T(1,128)S(1)} %bitcast.25), channel_id=1, replica_groups={{0,16,32,48,64,80,96,112},{128,144,160,176,192,208,224,240},{256,272,28..., dimensions={0} | all-to-all | bytes 425984 | tf_op jit(solution)/shard_map/all_to_all | solution.py:235
  64.9 13.2 %all_to_all.28 = f32[4,52,1,128]{3,2,1,0:T(1,128)S(1)} all-to-all(f32[4,52,1,128]{3,2,1,0:T(1,128)S(1)} %bitcast.23), channel_id=1, replica_groups={{0,128,256,384},{16,144,272,400},{32,160,288,416},{48,176,304,432},{64,..., dimensions={0} | all-to-all | bytes 212992 | tf_op jit(solution)/shard_map/all_to_all | solution.py:235
  78.1 10.0 %all_to_all.29 = f32[8,52,1,128]{3,2,1,0:T(1,128)S(1)} all-to-all(f32[8,52,1,128]{3,2,1,0:T(1,128)S(1)} %bitcast.21), channel_id=1, replica_groups={{0,16,32,48,64,80,96,112},{128,144,160,176,192,208,224,240},{256,272,28..., dimensions={0} | all-to-all | bytes 425984 | tf_op jit(solution)/shard_map/all_to_all | solution.py:235
  88.1 0.7 finish.1
  (4 shorter events, 0.1 us)
Async XLA Ops:
  3.3 42.5 %copy-start = (bf16[2048,768]{1,0:T(8,128)(2,1)S(1)}, bf16[2048,768]{1,0:T(8,128)(2,1)}, u32[]{:S(2)}) copy-start(bf16[2048,768]{1,0:T(8,128)(2,1)} %attempts_ref.1) | copy-start | bytes 9437188
  3.3 42.5 %copy-start.1 = (f32[64,64]{1,0:T(8,128)S(1)}, f32[64,64]{1,0:T(8,128)}, u32[]{:S(2)}) copy-start(f32[64,64]{1,0:T(8,128)} %core_ref.1) | copy-start | bytes 49156
  3.3 42.5 %copy-start.2 = (f32[4,64]{1,0:T(4,128)S(1)}, f32[4,64]{1,0:T(4,128)}, u32[]{:S(2)}) copy-start(f32[4,64]{1,0:T(4,128)} %weights_ref.1) | copy-start | bytes 3076
  3.3 42.5 %copy-start.3 = (s32[1,4]{1,0:T(1,128)S(1)}, s32[1,4]{1,0:T(1,128)}, u32[]{:S(2)}) copy-start(s32[1,4]{1,0:T(1,128)} %counts_ref.1) | copy-start | bytes 52

commit v8 on v7

--- a/solution.py
+++ b/solution.py
@@ -11,9 +11,9 @@
 NS_STEPS = 6
 PROJECT_VMEM = 56 * 1024 * 1024
 BLOCK = 128
-NEAR_ITEM = 4
-NEAR_STU = 8
-RING = (0, 1, 2, 3)
+NEAR_ITEM = (0, 1, 3, 2)
+NEAR_STU = (0, 1, 2, 3, 4, 5, 6, 7)
+N_FAR = 4
 F32 = jnp.float32
 BF16 = jnp.bfloat16
 NN = (((1,), (0,)), ((), ()))
@@ -235,17 +235,17 @@
     return lax.all_to_all(parted, axis, 0, 0, tiled=True, axis_index_groups=groups).reshape(rows.shape)
 
 
-def sum_over(axis, n_near, rows, gather):
-    n_far = len(RING)
-    near = [[far * n_near + i for i in range(n_near)] for far in range(n_far)]
-    distant = [[far * n_near + i for far in RING] for i in range(n_near)]
+def sum_over(axis, order, rows, gather):
+    n_near = len(order)
+    near = [[far * n_near + i for i in order] for far in range(N_FAR)]
+    distant = [[far * n_near + i for far in range(N_FAR)] for i in range(n_near)]
     rows = exchange(rows, n_near, axis, near)
     if gather:
         share = add_and_copy(rows, n_near, 1, "add_near_" + axis)
         rows = lax.all_gather(share, axis, axis_index_groups=distant, tiled=True)
     else:
-        rows = exchange(add_and_copy(rows, n_near, n_far, "add_near_" + axis), n_far, axis, distant)
-    return exchange(add_and_copy(rows, n_far, n_near, "add_far_" + axis), n_near, axis, near)
+        rows = exchange(add_and_copy(rows, n_near, N_FAR, "add_near_" + axis), N_FAR, axis, distant)
+    return exchange(add_and_copy(rows, N_FAR, n_near, "add_far_" + axis), n_near, axis, near)
 
 
 def local(n_stu, attempts, item_factor, core_factor, student_weights, blocks):

time: 89.1 us -> 88.8 us (level)
  no operation moved by 1% of the time
where the time goes in v8:
time: 88.8 us; the launch traced here: 88.5 us
  blocking collectives  79.2 us (89%)
  Pallas kernels  8.59 us (10%)
    all_to_all x5, blocking collectives, exchange(): lax.all_to_all(parted, axis, 0, 0, tiled=True, axis_index_groups=groups)  57.9 us
    all_gather x1, blocking collectives, sum_over(): rows = lax.all_gather(share, axis, axis_index_groups=distant, tiled=True)  21.2 us
    pallas_call x1, Pallas kernels, solve(): pl.pallas_call(solve_kernel, in_specs=[VMEM, VMEM, VMEM, SMEM, VMEM], out...  5.16 us
    pallas_call x1, Pallas kernels, project(): pl.pallas_call(project_kernel, in_specs=[pl.BlockSpec(memory_space=pl.ANY...  2.63 us

profile of v8, /device:TPU:1, one launch (start us, length us, event | category | flops | bytes accessed | tf_op | source)
XLA Modules:
  0.0 88.5 jit_solution(13423636762403877403)
XLA Ops:
  0.6 2.6 %project.1 = f32[16,64,128]{2,1,0:T(8,128)S(1)} custom-call(bf16[64,768]{1,0:T(8,128)(2,1)} %bitcast.26, bf16[2048,768]{1,0:T(8,128)(2,1)} %attempts_ref.1), custom_call_target="tpu_custom_call" | custom-call | tf_op jit(solution)/shard_map/project/pallas_call | solution.py:48
  3.3 0.0 copy-start
  3.3 0.0 copy-start.1
  3.3 0.0 copy-start.2
  3.3 0.0 copy-start.3
  3.3 11.5 %all_to_all.25 = f32[4,256,1,128]{3,1,2,0:T(8,128)S(1)} all-to-all(f32[4,256,1,128]{3,1,2,0:T(8,128)S(1)} %bitcast.17), channel_id=1, replica_groups={{0,1,3,2},{4,5,7,6},{8,9,11,10},{12,13,15,14},{16,17,19,18},{20,21,23,2..., dimensions={0} | all-to-all | bytes 1048576 | tf_op jit(solution)/shard_map/all_to_all | solution.py:235
  14.9 21.2 %all_gather.3.in_ref = f32[1024,128]{1,0:T(8,128)S(1)} all-gather(f32[256,128]{1,0:T(8,128)S(1)} %add_near_item.1), channel_id=1, replica_groups={{0,4,8,12},{1,5,9,13},{2,6,10,14},{3,7,11,15},{16,20,24,28},{17,21,25,2..., dimensions={0}, use_global_device_ids=true | all-gather | bytes 655360 | tf_op jit(solution)/shard_map/all_gather | solution.py:245
  36.2 9.0 %all_to_all.26 = f32[4,256,1,128]{3,1,2,0:T(8,128)S(1)} all-to-all(f32[4,256,1,128]{3,1,2,0:T(8,128)S(1)} %bitcast.19), channel_id=1, replica_groups={{0,1,3,2},{4,5,7,6},{8,9,11,10},{12,13,15,14},{16,17,19,18},{20,21,23,2..., dimensions={0} | all-to-all | bytes 1048576 | tf_op jit(solution)/shard_map/all_to_all | solution.py:235
  45.2 0.0 copy-done
  45.2 0.0 copy-done.1
  45.2 0.0 copy-done.2
  45.2 0.0 copy-done.3
  45.2 5.2 %solve.1 = (f32[416,128]{1,0:T(8,128)S(1)}, f32[4,64]{1,0:T(4,128)}) custom-call(f32[16,64,128]{2,1,0:T(8,128)S(1)} %bitcast.16, f32[64,64]{1,0:T(8,128)S(1)} %copy-done.1, f32[4,64]{1,0:T(4,128)S(1)} %copy-done.2, s32[1,4]{1,0:T(1,128)S(1)} %copy-done.3, bf16[2048,768]{1,0:T(8,128)(2,1)S(1)} %copy-done), custom_call_target="tpu_custom_call" | custom-call | tf_op jit(solution)/shard_map/solve/pallas_call | solution.py:191
  50.4 13.9 %all_to_all.27 = f32[8,52,1,128]{3,2,1,0:T(1,128)S(1)} all-to-all(f32[8,52,1,128]{3,2,1,0:T(1,128)S(1)} %bitcast.25), channel_id=1, replica_groups={{0,16,32,48,64,80,96,112},{128,144,160,176,192,208,224,240},{256,272,28..., dimensions={0} | all-to-all | bytes 425984 | tf_op jit(solution)/shard_map/all_to_all | solution.py:235
  64.3 13.5 %all_to_all.28 = f32[4,52,1,128]{3,2,1,0:T(1,128)S(1)} all-to-all(f32[4,52,1,128]{3,2,1,0:T(1,128)S(1)} %bitcast.23), channel_id=1, replica_groups={{0,128,256,384},{16,144,272,400},{32,160,288,416},{48,176,304,432},{64,..., dimensions={0} | all-to-all | bytes 212992 | tf_op jit(solution)/shard_map/all_to_all | solution.py:235
  77.8 10.0 %all_to_all.29 = f32[8,52,1,128]{3,2,1,0:T(1,128)S(1)} all-to-all(f32[8,52,1,128]{3,2,1,0:T(1,128)S(1)} %bitcast.21), channel_id=1, replica_groups={{0,16,32,48,64,80,96,112},{128,144,160,176,192,208,224,240},{256,272,28..., dimensions={0} | all-to-all | bytes 425984 | tf_op jit(solution)/shard_map/all_to_all | solution.py:235
  87.8 0.7 finish.1
  (4 shorter events, 0.1 us)
Async XLA Ops:
  3.3 41.9 %copy-start = (bf16[2048,768]{1,0:T(8,128)(2,1)S(1)}, bf16[2048,768]{1,0:T(8,128)(2,1)}, u32[]{:S(2)}) copy-start(bf16[2048,768]{1,0:T(8,128)(2,1)} %attempts_ref.1) | copy-start | bytes 9437188
  3.3 41.9 %copy-start.1 = (f32[64,64]{1,0:T(8,128)S(1)}, f32[64,64]{1,0:T(8,128)}, u32[]{:S(2)}) copy-start(f32[64,64]{1,0:T(8,128)} %core_ref.1) | copy-start | bytes 49156
  3.3 41.9 %copy-start.2 = (f32[4,64]{1,0:T(4,128)S(1)}, f32[4,64]{1,0:T(4,128)}, u32[]{:S(2)}) copy-start(f32[4,64]{1,0:T(4,128)} %weights_ref.1) | copy-start | bytes 3076
  3.3 41.9 %copy-start.3 = (s32[1,4]{1,0:T(1,128)S(1)}, s32[1,4]{1,0:T(1,128)}, u32[]{:S(2)}) copy-start(s32[1,4]{1,0:T(1,128)} %counts_ref.1) | copy-start | bytes 52

commit v9 on v8

--- a/solution.py
+++ b/solution.py
@@ -152,15 +152,18 @@
         inverse = 1.0 / jnp.sqrt(jnp.where(on_left, left_trace, right_trace) + 1e-06)
         gram.append(times(half_way, lift_t_right[pair]) * (inverse * inverse))
         polynomial.append(lift_t[pair] * inverse)
-    for iteration in range(NS_STEPS):
-        factor = [right(1.5 * identity - 0.5 * gram[pair]) for pair in pairs]
-        if iteration < NS_STEPS - 1:
-            moved = [times(gram[pair], factor[pair]) for pair in pairs]
-            gram = [times(moved[pair], factor[pair]) for pair in pairs]
-        polynomial = [times(polynomial[pair], factor[pair]) for pair in pairs]
-
-    apply = beside([times(polynomial[pair], lift_right[pair]) for pair in pairs])
-    polynomial = beside(polynomial)
+    for iteration in range(NS_STEPS - 1):
+        factor = [1.5 * identity - 0.5 * gram[pair] for pair in pairs]
+        factor_right = [right(factor[pair]) for pair in pairs]
+        moved = [times(gram[pair], factor_right[pair]) for pair in pairs]
+        if iteration < NS_STEPS - 2:
+            gram = [times(moved[pair], factor_right[pair]) for pair in pairs]
+        polynomial = [times(polynomial[pair], factor_right[pair]) for pair in pairs]
+    ahead = [right(times(factor[pair], lift_right[pair])) for pair in pairs]
+    bent = [times(polynomial[pair], right(moved[pair])) for pair in pairs]
+    straight = [times(polynomial[pair], lift_right[pair]) for pair in pairs]
+    apply = beside([1.5 * straight[pair] - 0.5 * times(bent[pair], ahead[pair]) for pair in pairs])
+    polynomial = beside([1.5 * polynomial[pair] - 0.5 * times(bent[pair], factor_right[pair]) for pair in pairs])
     for student in range(students):
         high, low = split(apply[:, student * rank : (student + 1) * rank])
         lifts[student] = jnp.concatenate([beside([high, high]), beside([low, low])], axis=0)

time: 88.8 us -> 88.7 us (level)
  no operation moved by 1% of the time
where the time goes in v9:
time: 88.7 us; the launch traced here: 88.4 us
  blocking collectives  79.2 us (89%)
  Pallas kernels  8.46 us (10%)
    all_to_all x5, blocking collectives, exchange(): lax.all_to_all(parted, axis, 0, 0, tiled=True, axis_index_groups=groups)  57.9 us
    all_gather x1, blocking collectives, sum_over(): rows = lax.all_gather(share, axis, axis_index_groups=distant, tiled=True)  21.2 us
    pallas_call x1, Pallas kernels, solve(): pl.pallas_call(solve_kernel, in_specs=[VMEM, VMEM, VMEM, SMEM, VMEM], out...  5.03 us
    pallas_call x1, Pallas kernels, project(): pl.pallas_call(project_kernel, in_specs=[pl.BlockSpec(memory_space=pl.ANY...  2.63 us

profile of v9, /device:TPU:1, one launch (start us, length us, event | category | flops | bytes accessed | tf_op | source)
XLA Modules:
  0.0 88.4 jit_solution(7852870343806141003)
XLA Ops:
  0.6 2.6 %project.1 = f32[16,64,128]{2,1,0:T(8,128)S(1)} custom-call(bf16[64,768]{1,0:T(8,128)(2,1)} %bitcast.26, bf16[2048,768]{1,0:T(8,128)(2,1)} %attempts_ref.1), custom_call_target="tpu_custom_call" | custom-call | tf_op jit(solution)/shard_map/project/pallas_call | solution.py:48
  3.3 0.0 copy-start
  3.3 0.0 copy-start.1
  3.3 0.0 copy-start.2
  3.3 0.0 copy-start.3
  3.3 11.5 %all_to_all.25 = f32[4,256,1,128]{3,1,2,0:T(8,128)S(1)} all-to-all(f32[4,256,1,128]{3,1,2,0:T(8,128)S(1)} %bitcast.17), channel_id=1, replica_groups={{0,1,3,2},{4,5,7,6},{8,9,11,10},{12,13,15,14},{16,17,19,18},{20,21,23,2..., dimensions={0} | all-to-all | bytes 1048576 | tf_op jit(solution)/shard_map/all_to_all | solution.py:238
  14.9 21.2 %all_gather.3.in_ref = f32[1024,128]{1,0:T(8,128)S(1)} all-gather(f32[256,128]{1,0:T(8,128)S(1)} %add_near_item.1), channel_id=1, replica_groups={{0,4,8,12},{1,5,9,13},{2,6,10,14},{3,7,11,15},{16,20,24,28},{17,21,25,2..., dimensions={0}, use_global_device_ids=true | all-gather | bytes 655360 | tf_op jit(solution)/shard_map/all_gather | solution.py:248
  36.2 9.0 %all_to_all.26 = f32[4,256,1,128]{3,1,2,0:T(8,128)S(1)} all-to-all(f32[4,256,1,128]{3,1,2,0:T(8,128)S(1)} %bitcast.19), channel_id=1, replica_groups={{0,1,3,2},{4,5,7,6},{8,9,11,10},{12,13,15,14},{16,17,19,18},{20,21,23,2..., dimensions={0} | all-to-all | bytes 1048576 | tf_op jit(solution)/shard_map/all_to_all | solution.py:238
  45.2 0.0 copy-done
  45.2 0.0 copy-done.1
  45.2 0.0 copy-done.2
  45.2 0.0 copy-done.3
  45.2 5.0 %solve.1 = (f32[416,128]{1,0:T(8,128)S(1)}, f32[4,64]{1,0:T(4,128)}) custom-call(f32[16,64,128]{2,1,0:T(8,128)S(1)} %bitcast.16, f32[64,64]{1,0:T(8,128)S(1)} %copy-done.1, f32[4,64]{1,0:T(4,128)S(1)} %copy-done.2, s32[1,4]{1,0:T(1,128)S(1)} %copy-done.3, bf16[2048,768]{1,0:T(8,128)(2,1)S(1)} %copy-done), custom_call_target="tpu_custom_call" | custom-call | tf_op jit(solution)/shard_map/solve/pallas_call | solution.py:194
  50.3 13.9 %all_to_all.27 = f32[8,52,1,128]{3,2,1,0:T(1,128)S(1)} all-to-all(f32[8,52,1,128]{3,2,1,0:T(1,128)S(1)} %bitcast.25), channel_id=1, replica_groups={{0,16,32,48,64,80,96,112},{128,144,160,176,192,208,224,240},{256,272,28..., dimensions={0} | all-to-all | bytes 425984 | tf_op jit(solution)/shard_map/all_to_all | solution.py:238
  64.2 13.5 %all_to_all.28 = f32[4,52,1,128]{3,2,1,0:T(1,128)S(1)} all-to-all(f32[4,52,1,128]{3,2,1,0:T(1,128)S(1)} %bitcast.23), channel_id=1, replica_groups={{0,128,256,384},{16,144,272,400},{32,160,288,416},{48,176,304,432},{64,..., dimensions={0} | all-to-all | bytes 212992 | tf_op jit(solution)/shard_map/all_to_all | solution.py:238
  77.7 10.0 %all_to_all.29 = f32[8,52,1,128]{3,2,1,0:T(1,128)S(1)} all-to-all(f32[8,52,1,128]{3,2,1,0:T(1,128)S(1)} %bitcast.21), channel_id=1, replica_groups={{0,16,32,48,64,80,96,112},{128,144,160,176,192,208,224,240},{256,272,28..., dimensions={0} | all-to-all | bytes 425984 | tf_op jit(solution)/shard_map/all_to_all | solution.py:238
  87.7 0.7 finish.1
  (4 shorter events, 0.1 us)
Async XLA Ops:
  3.3 41.9 %copy-start = (bf16[2048,768]{1,0:T(8,128)(2,1)S(1)}, bf16[2048,768]{1,0:T(8,128)(2,1)}, u32[]{:S(2)}) copy-start(bf16[2048,768]{1,0:T(8,128)(2,1)} %attempts_ref.1) | copy-start | bytes 9437188
  3.3 41.9 %copy-start.1 = (f32[64,64]{1,0:T(8,128)S(1)}, f32[64,64]{1,0:T(8,128)}, u32[]{:S(2)}) copy-start(f32[64,64]{1,0:T(8,128)} %core_ref.1) | copy-start | bytes 49156
  3.3 41.9 %copy-start.2 = (f32[4,64]{1,0:T(4,128)S(1)}, f32[4,64]{1,0:T(4,128)}, u32[]{:S(2)}) copy-start(f32[4,64]{1,0:T(4,128)} %weights_ref.1) | copy-start | bytes 3076
  3.3 41.9 %copy-start.3 = (s32[1,4]{1,0:T(1,128)S(1)}, s32[1,4]{1,0:T(1,128)}, u32[]{:S(2)}) copy-start(s32[1,4]{1,0:T(1,128)} %counts_ref.1) | copy-start | bytes 52

commit v10 on v9

--- a/solution.py
+++ b/solution.py
@@ -186,6 +186,9 @@
         parts_ref[tile * rank : (tile + 1) * rank, :] = item_part[:, tile * BLOCK : (tile + 1) * BLOCK]
     last = tiles * rank
     parts_ref[last : last + rank // 2, :] = beside([shared[: rank // 2], shared[rank // 2 :]])
+    used = last + rank // 2
+    if parts_ref.shape[0] > used:
+        parts_ref[used:, :] = jnp.zeros((parts_ref.shape[0] - used, BLOCK), F32)
 
 
 def solve(raw, core_factor, student_weights, blocks, attempts, part_rows):
@@ -251,12 +254,13 @@
     return exchange(add_and_copy(rows, N_FAR, n_near, "add_far_" + axis), n_near, axis, near)
 
 
-def local(n_stu, attempts, item_factor, core_factor, student_weights, blocks):
+def local(attempts, item_factor, core_factor, student_weights, blocks):
     items, rank = item_factor.shape
     sums = project(attempts, item_factor.T, 2)
     raw = sum_over("item", NEAR_ITEM, sums.reshape(-1, BLOCK), True).reshape(sums.shape)
     used = items // BLOCK * rank + rank // 2
-    parts, student_part = solve(raw, core_factor, student_weights, blocks, attempts, -(-used // n_stu) * n_stu)
+    step = 8 * len(NEAR_STU)
+    parts, student_part = solve(raw, core_factor, student_weights, blocks, attempts, -(-used // step) * step)
     item_total, shared_total = finish(sum_over("stu", NEAR_STU, parts, False), rank, items)
     return (item_total.T, shared_total, student_part)
 
@@ -264,5 +268,4 @@
 def solution(mesh):
     in_specs = (P("stu", "item"), P("item", None), P(), P("stu", None), P("stu", None))
     out_specs = (P("item", None), P(), P("stu", None))
-    body = functools.partial(local, mesh.shape["stu"])
-    return jax.shard_map(body, mesh=mesh, in_specs=in_specs, out_specs=out_specs, check_vma=False)
+    return jax.shard_map(local, mesh=mesh, in_specs=in_specs, out_specs=out_specs, check_vma=False)

time: 88.7 us -> 89 us (level)
  no operation moved by 1% of the time
where the time goes in v10:
time: 89 us; the launch traced here: 88.7 us
  blocking collectives  79.5 us (89%)
  Pallas kernels  8.45 us (9%)
    all_to_all x5, blocking collectives, exchange(): lax.all_to_all(parted, axis, 0, 0, tiled=True, axis_index_groups=groups)  58.3 us
    all_gather x1, blocking collectives, sum_over(): rows = lax.all_gather(share, axis, axis_index_groups=distant, tiled=True)  21.2 us
    pallas_call x1, Pallas kernels, solve(): pl.pallas_call(solve_kernel, in_specs=[VMEM, VMEM, VMEM, SMEM, VMEM], out...  5.02 us
    pallas_call x1, Pallas kernels, project(): pl.pallas_call(project_kernel, in_specs=[pl.BlockSpec(memory_space=pl.ANY...  2.63 us

profile of v10, /device:TPU:1, one launch (start us, length us, event | category | flops | bytes accessed | tf_op | source)
XLA Modules:
  0.0 88.7 jit_solution(5439795275336936203)
XLA Ops:
  0.6 2.6 %project.1 = f32[16,64,128]{2,1,0:T(8,128)S(1)} custom-call(bf16[64,768]{1,0:T(8,128)(2,1)} %bitcast.32, bf16[2048,768]{1,0:T(8,128)(2,1)} %attempts_ref.1), custom_call_target="tpu_custom_call" | custom-call | tf_op jit(solution)/shard_map/project/pallas_call | solution.py:48
  3.3 0.0 copy-start
  3.3 0.0 copy-start.1
  3.3 0.0 copy-start.2
  3.3 0.0 copy-start.3
  3.3 11.5 %all_to_all.25 = f32[4,256,1,128]{3,1,2,0:T(8,128)S(1)} all-to-all(f32[4,256,1,128]{3,1,2,0:T(8,128)S(1)} %bitcast.23), channel_id=1, replica_groups={{0,1,3,2},{4,5,7,6},{8,9,11,10},{12,13,15,14},{16,17,19,18},{20,21,23,2..., dimensions={0} | all-to-all | bytes 1048576 | tf_op jit(solution)/shard_map/all_to_all | solution.py:241
  14.9 21.2 %all_gather.3.in_ref = f32[1024,128]{1,0:T(8,128)S(1)} all-gather(f32[256,128]{1,0:T(8,128)S(1)} %add_near_item.1), channel_id=1, replica_groups={{0,4,8,12},{1,5,9,13},{2,6,10,14},{3,7,11,15},{16,20,24,28},{17,21,25,2..., dimensions={0}, use_global_device_ids=true | all-gather | bytes 655360 | tf_op jit(solution)/shard_map/all_gather | solution.py:251
  36.2 9.0 %all_to_all.26 = f32[4,256,1,128]{3,1,2,0:T(8,128)S(1)} all-to-all(f32[4,256,1,128]{3,1,2,0:T(8,128)S(1)} %bitcast.25), channel_id=1, replica_groups={{0,1,3,2},{4,5,7,6},{8,9,11,10},{12,13,15,14},{16,17,19,18},{20,21,23,2..., dimensions={0} | all-to-all | bytes 1048576 | tf_op jit(solution)/shard_map/all_to_all | solution.py:241
  45.2 0.0 copy-done
  45.2 0.0 copy-done.1
  45.2 0.0 copy-done.2
  45.2 0.0 copy-done.3
  45.2 5.0 %solve.1 = (f32[448,128]{1,0:T(8,128)S(1)}, f32[4,64]{1,0:T(4,128)}) custom-call(f32[16,64,128]{2,1,0:T(8,128)S(1)} %bitcast.22, f32[64,64]{1,0:T(8,128)S(1)} %copy-done.1, f32[4,64]{1,0:T(4,128)S(1)} %copy-done.2, s32[1,4]{1,0:T(1,128)S(1)} %copy-done.3, bf16[2048,768]{1,0:T(8,128)(2,1)S(1)} %copy-done), custom_call_target="tpu_custom_call" | custom-call | tf_op jit(solution)/shard_map/solve/pallas_call | solution.py:197
  50.3 14.1 %all_to_all.27 = f32[8,56,1,128]{3,1,2,0:T(8,128)S(1)} all-to-all(f32[8,56,1,128]{3,1,2,0:T(8,128)S(1)} %bitcast.31), channel_id=1, replica_groups={{0,16,32,48,64,80,96,112},{128,144,160,176,192,208,224,240},{256,272,28..., dimensions={0} | all-to-all | bytes 458752 | tf_op jit(solution)/shard_map/all_to_all | solution.py:241
  64.4 13.5 %all_to_all.28 = f32[4,56,1,128]{3,1,2,0:T(8,128)S(1)} all-to-all(f32[4,56,1,128]{3,1,2,0:T(8,128)S(1)} %bitcast.29), channel_id=1, replica_groups={{0,128,256,384},{16,144,272,400},{32,160,288,416},{48,176,304,432},{64,..., dimensions={0} | all-to-all | bytes 229376 | tf_op jit(solution)/shard_map/all_to_all | solution.py:241
  77.9 10.1 %all_to_all.29 = f32[8,56,1,128]{3,1,2,0:T(8,128)S(1)} all-to-all(f32[8,56,1,128]{3,1,2,0:T(8,128)S(1)} %bitcast.28), channel_id=1, replica_groups={{0,16,32,48,64,80,96,112},{128,144,160,176,192,208,224,240},{256,272,28..., dimensions={0} | all-to-all | bytes 458752 | tf_op jit(solution)/shard_map/all_to_all | solution.py:241
  88.0 0.7 finish.1
  (4 shorter events, 0.1 us)
Async XLA Ops:
  3.3 41.9 %copy-start = (bf16[2048,768]{1,0:T(8,128)(2,1)S(1)}, bf16[2048,768]{1,0:T(8,128)(2,1)}, u32[]{:S(2)}) copy-start(bf16[2048,768]{1,0:T(8,128)(2,1)} %attempts_ref.1) | copy-start | bytes 9437188
  3.3 41.9 %copy-start.1 = (f32[64,64]{1,0:T(8,128)S(1)}, f32[64,64]{1,0:T(8,128)}, u32[]{:S(2)}) copy-start(f32[64,64]{1,0:T(8,128)} %core_ref.1) | copy-start | bytes 49156
  3.3 41.9 %copy-start.2 = (f32[4,64]{1,0:T(4,128)S(1)}, f32[4,64]{1,0:T(4,128)}, u32[]{:S(2)}) copy-start(f32[4,64]{1,0:T(4,128)} %weights_ref.1) | copy-start | bytes 3076
  3.3 41.9 %copy-start.3 = (s32[1,4]{1,0:T(1,128)S(1)}, s32[1,4]{1,0:T(1,128)}, u32[]{:S(2)}) copy-start(s32[1,4]{1,0:T(1,128)} %counts_ref.1) | copy-start | bytes 52

commit v11 on v9

--- a/solution.py
+++ b/solution.py
@@ -14,6 +14,7 @@
 NEAR_ITEM = (0, 1, 3, 2)
 NEAR_STU = (0, 1, 2, 3, 4, 5, 6, 7)
 N_FAR = 4
+RING = (0, 1, 3, 2)
 F32 = jnp.float32
 BF16 = jnp.bfloat16
 NN = (((1,), (0,)), ((), ()))
@@ -241,7 +242,7 @@
 def sum_over(axis, order, rows, gather):
     n_near = len(order)
     near = [[far * n_near + i for i in order] for far in range(N_FAR)]
-    distant = [[far * n_near + i for far in range(N_FAR)] for i in range(n_near)]
+    distant = [[far * n_near + i for far in (range(N_FAR) if gather else RING)] for i in range(n_near)]
     rows = exchange(rows, n_near, axis, near)
     if gather:
         share = add_and_copy(rows, n_near, 1, "add_near_" + axis)

time: 88.7 us -> 88.1 us (level)
  no operation moved by 1% of the time
where the time goes in v11:
time: 88.1 us; the launch traced here: 87.8 us
  blocking collectives  78.7 us (89%)
  Pallas kernels  8.45 us (10%)
    all_to_all x5, blocking collectives, exchange(): lax.all_to_all(parted, axis, 0, 0, tiled=True, axis_index_groups=groups)  57.4 us
    all_gather x1, blocking collectives, sum_over(): rows = lax.all_gather(share, axis, axis_index_groups=distant, tiled=True)  21.2 us
    pallas_call x1, Pallas kernels, solve(): pl.pallas_call(solve_kernel, in_specs=[VMEM, VMEM, VMEM, SMEM, VMEM], out...  5.02 us
    pallas_call x1, Pallas kernels, project(): pl.pallas_call(project_kernel, in_specs=[pl.BlockSpec(memory_space=pl.ANY...  2.63 us

profile of v11, /device:TPU:1, one launch (start us, length us, event | category | flops | bytes accessed | tf_op | source)
XLA Modules:
  0.0 87.8 jit_solution(2942489582171580997)
XLA Ops:
  0.6 2.6 %project.1 = f32[16,64,128]{2,1,0:T(8,128)S(1)} custom-call(bf16[64,768]{1,0:T(8,128)(2,1)} %bitcast.26, bf16[2048,768]{1,0:T(8,128)(2,1)} %attempts_ref.1), custom_call_target="tpu_custom_call" | custom-call | tf_op jit(solution)/shard_map/project/pallas_call | solution.py:49
  3.3 0.0 copy-start
  3.3 0.0 copy-start.1
  3.3 0.0 copy-start.2
  3.3 0.0 copy-start.3
  3.3 11.5 %all_to_all.25 = f32[4,256,1,128]{3,1,2,0:T(8,128)S(1)} all-to-all(f32[4,256,1,128]{3,1,2,0:T(8,128)S(1)} %bitcast.17), channel_id=1, replica_groups={{0,1,3,2},{4,5,7,6},{8,9,11,10},{12,13,15,14},{16,17,19,18},{20,21,23,2..., dimensions={0} | all-to-all | bytes 1048576 | tf_op jit(solution)/shard_map/all_to_all | solution.py:239
  14.9 21.2 %all_gather.3.in_ref = f32[1024,128]{1,0:T(8,128)S(1)} all-gather(f32[256,128]{1,0:T(8,128)S(1)} %add_near_item.1), channel_id=1, replica_groups={{0,4,8,12},{1,5,9,13},{2,6,10,14},{3,7,11,15},{16,20,24,28},{17,21,25,2..., dimensions={0}, use_global_device_ids=true | all-gather | bytes 655360 | tf_op jit(solution)/shard_map/all_gather | solution.py:249
  36.2 9.0 %all_to_all.26 = f32[4,256,1,128]{3,1,2,0:T(8,128)S(1)} all-to-all(f32[4,256,1,128]{3,1,2,0:T(8,128)S(1)} %bitcast.19), channel_id=1, replica_groups={{0,1,3,2},{4,5,7,6},{8,9,11,10},{12,13,15,14},{16,17,19,18},{20,21,23,2..., dimensions={0} | all-to-all | bytes 1048576 | tf_op jit(solution)/shard_map/all_to_all | solution.py:239
  45.2 0.0 copy-done
  45.2 0.0 copy-done.1
  45.2 0.0 copy-done.2
  45.2 0.0 copy-done.3
  45.2 5.0 %solve.1 = (f32[416,128]{1,0:T(8,128)S(1)}, f32[4,64]{1,0:T(4,128)}) custom-call(f32[16,64,128]{2,1,0:T(8,128)S(1)} %bitcast.16, f32[64,64]{1,0:T(8,128)S(1)} %copy-done.1, f32[4,64]{1,0:T(4,128)S(1)} %copy-done.2, s32[1,4]{1,0:T(1,128)S(1)} %copy-done.3, bf16[2048,768]{1,0:T(8,128)(2,1)S(1)} %copy-done), custom_call_target="tpu_custom_call" | custom-call | tf_op jit(solution)/shard_map/solve/pallas_call | solution.py:195
  50.2 14.0 %all_to_all.27 = f32[8,52,1,128]{3,2,1,0:T(1,128)S(1)} all-to-all(f32[8,52,1,128]{3,2,1,0:T(1,128)S(1)} %bitcast.25), channel_id=1, replica_groups={{0,16,32,48,64,80,96,112},{128,144,160,176,192,208,224,240},{256,272,28..., dimensions={0} | all-to-all | bytes 425984 | tf_op jit(solution)/shard_map/all_to_all | solution.py:239
  64.2 13.3 %all_to_all.28 = f32[4,52,1,128]{3,2,1,0:T(1,128)S(1)} all-to-all(f32[4,52,1,128]{3,2,1,0:T(1,128)S(1)} %bitcast.23), channel_id=1, replica_groups={{0,128,384,256},{16,144,400,272},{32,160,416,288},{48,176,432,304},{64,..., dimensions={0} | all-to-all | bytes 212992 | tf_op jit(solution)/shard_map/all_to_all | solution.py:239
  77.5 9.6 %all_to_all.29 = f32[8,52,1,128]{3,2,1,0:T(1,128)S(1)} all-to-all(f32[8,52,1,128]{3,2,1,0:T(1,128)S(1)} %bitcast.21), channel_id=1, replica_groups={{0,16,32,48,64,80,96,112},{128,144,160,176,192,208,224,240},{256,272,28..., dimensions={0} | all-to-all | bytes 425984 | tf_op jit(solution)/shard_map/all_to_all | solution.py:239
  87.1 0.7 finish.1
  (4 shorter events, 0.1 us)
Async XLA Ops:
  3.3 41.9 %copy-start = (bf16[2048,768]{1,0:T(8,128)(2,1)S(1)}, bf16[2048,768]{1,0:T(8,128)(2,1)}, u32[]{:S(2)}) copy-start(bf16[2048,768]{1,0:T(8,128)(2,1)} %attempts_ref.1) | copy-start | bytes 9437188
  3.3 41.9 %copy-start.1 = (f32[64,64]{1,0:T(8,128)S(1)}, f32[64,64]{1,0:T(8,128)}, u32[]{:S(2)}) copy-start(f32[64,64]{1,0:T(8,128)} %core_ref.1) | copy-start | bytes 49156
  3.3 41.9 %copy-start.2 = (f32[4,64]{1,0:T(4,128)S(1)}, f32[4,64]{1,0:T(4,128)}, u32[]{:S(2)}) copy-start(f32[4,64]{1,0:T(4,128)} %weights_ref.1) | copy-start | bytes 3076
  3.3 41.9 %copy-start.3 = (s32[1,4]{1,0:T(1,128)S(1)}, s32[1,4]{1,0:T(1,128)}, u32[]{:S(2)}) copy-start(s32[1,4]{1,0:T(1,128)} %counts_ref.1) | copy-start | bytes 52
